TPU v7x, 128 devices: a whole 4x4x4 slice. The times are simulated.
128 devices in a mesh: rows: 8 (over z_lo, x), cols: 16 (over y, z_hi, core).
Axes of the slice: x: 4, y: 4, z: 4 (z_hi: 2, z_lo: 2; z = z_hi * 2 + z_lo), core: 2. Of those that a mesh axis runs over, the one named last changes fastest.
Arguments:
- model: bfloat16 [256, 512, 512], P(('rows', 'cols')), may hold values from -6 to 6
- dirty: bfloat16 [256, 512, 512], P(('rows', 'cols')), may hold values from -6 to 6
- psf: bfloat16 [256, 256, 256], P(('rows', 'cols')), may hold values from -0.0234375 to 0.0234375
- step_size: float32 [256], P(('rows', 'cols')), may hold values from 0.2 to 1
- gain: float32 [256], replicated, may hold values from 0.1 to 1.9
- w_in: bfloat16 [256, 256], replicated, may hold values from -0.375 to 0.375
- b_in: float32 [256], replicated, may hold values from -3 to 3
- w_out: bfloat16 [256, 256], replicated, may hold values from -0.375 to 0.375
- kernel: float32 [3, 3, 256], replicated, may hold values from -2 to 2
Outputs:
- updated_model: bfloat16 [256, 512, 512], P(('rows', 'cols'))
All inputs are finite; a program needn't handle non-finite values.
Results may differ from a plain program's by a relative error of at most 0.0095.
Values may be sent and summed in bfloat16 or wider, within the bound.
A program may use at most 64 MiB of HBM per device.

v0:
```python
import math

import jax
import jax.numpy as jnp
from jax import lax
from jax.sharding import PartitionSpec as P

FFT = 1024


def padded_2(block, sides, width):
    for axis, dim in sides:
        count = lax.axis_size(axis)
        forward = [(i, i + 1) for i in range(count - 1)]
        backward = [(target, source) for source, target in forward]
        low = lax.ppermute(
            lax.slice_in_dim(block, block.shape[dim] - width, None, axis=dim), axis, forward
        )
        high = lax.ppermute(lax.slice_in_dim(block, 0, width, axis=dim), axis, backward)
        block = jnp.concatenate([low, block, high], axis=dim)
    return block


def tables(length, count, offset):
    freq = jnp.arange(length, dtype=jnp.int32)[:, None]
    place = jnp.arange(count, dtype=jnp.int32)[None, :] + offset
    phase = (freq * place % length).astype(jnp.float32) * (2.0 * math.pi / length)
    return (jnp.cos(phase).astype(jnp.bfloat16), jnp.sin(phase).astype(jnp.bfloat16))


def spectrum(plane, cos_t, sin_t):
    real_a = jnp.dot(cos_t, plane, preferred_element_type=jnp.float32).astype(jnp.bfloat16)
    imag_a = (-jnp.dot(sin_t, plane, preferred_element_type=jnp.float32)).astype(jnp.bfloat16)
    real_s = jnp.dot(real_a, cos_t.T, preferred_element_type=jnp.float32) + jnp.dot(
        imag_a, sin_t.T, preferred_element_type=jnp.float32
    )
    imag_s = jnp.dot(imag_a, cos_t.T, preferred_element_type=jnp.float32) - jnp.dot(
        real_a, sin_t.T, preferred_element_type=jnp.float32
    )
    return (real_s, imag_s)


def convolve(plane, spread_fn, image_tabs, psf_tabs, window_tabs, length):
    real_x, imag_x = spectrum(plane, image_tabs[0], image_tabs[1])
    real_q, imag_q = spectrum(spread_fn, psf_tabs[0], psf_tabs[1])
    factor = 1.0 / (length * length)
    real_p = ((real_x * real_q - imag_x * imag_q) * factor).astype(jnp.bfloat16)
    imag_p = ((real_x * imag_q + imag_x * real_q) * factor).astype(jnp.bfloat16)
    cos_w, sin_w = window_tabs
    real_b = (
        jnp.dot(real_p, cos_w, preferred_element_type=jnp.float32)
        - jnp.dot(imag_p, sin_w, preferred_element_type=jnp.float32)
    ).astype(jnp.bfloat16)
    imag_b = (
        jnp.dot(real_p, sin_w, preferred_element_type=jnp.float32)
        + jnp.dot(imag_p, cos_w, preferred_element_type=jnp.float32)
    ).astype(jnp.bfloat16)
    return jnp.dot(cos_w.T, real_b, preferred_element_type=jnp.float32) - jnp.dot(
        sin_w.T, imag_b, preferred_element_type=jnp.float32
    )


def prior_mix(pixels, gain, w_in, b_in, w_out):
    values = pixels.astype(jnp.float32)
    power = jnp.mean(values * values, axis=0, keepdims=True)
    normed = (values / jnp.sqrt(power + 1e-06) * gain[:, None]).astype(jnp.bfloat16)
    inner = jnp.dot(w_in.T, normed, preferred_element_type=jnp.float32) + b_in[:, None]
    hidden = jax.nn.gelu(inner, approximate=True).astype(jnp.bfloat16)
    return jnp.dot(w_out.T, hidden, preferred_element_type=jnp.float32).astype(jnp.bfloat16)


def spread(padded, kernel, height, width):
    total = jnp.zeros((padded.shape[0], height, width), jnp.float32)
    for row_tap in range(3):
        for col_tap in range(3):
            total = total + kernel[row_tap, col_tap][:, None, None] * padded[
                :, row_tap : row_tap + height, col_tap : col_tap + width
            ].astype(jnp.float32)
    return total


def to_tiles(blocks):
    pixels = blocks.shape[3]
    moved = lax.all_to_all(
        blocks.reshape(-1, pixels), ("rows", "cols"), split_axis=0, concat_axis=0, tiled=True
    )
    return moved


def to_planes(blocks):
    shape = blocks.shape
    moved = lax.all_to_all(
        blocks.reshape(-1, shape[3]), ("rows", "cols"), split_axis=0, concat_axis=0, tiled=True
    )
    return moved.reshape(shape)


def local(model, dirty, psf, step_size, gain, w_in, b_in, w_out, kernel):
    ch_dev = model.shape[0]
    img_len = model.shape[1]
    psf_len = psf.shape[1]
    image_tabs = tables(FFT, img_len, 0)
    psf_tabs = tables(FFT, psf_len, 0)
    window_tabs = tables(FFT, img_len, psf_len // 2)

    def one_channel(items):
        plane, dirty_plane, psf_plane, rate = items
        blurred = convolve(plane, psf_plane, image_tabs, psf_tabs, window_tabs, FFT)
        return (
            plane.astype(jnp.float32) + rate * (dirty_plane.astype(jnp.float32) - blurred)
        ).astype(jnp.bfloat16)

    stepped = lax.map(one_channel, (model, dirty, psf, step_size))
    n_rows = lax.axis_size("rows")
    n_cols = lax.axis_size("cols")
    tile_rows = img_len // n_rows
    tile_cols = img_len // n_cols
    blocks = stepped.reshape(ch_dev, n_rows, tile_rows, n_cols, tile_cols).transpose(1, 3, 0, 2, 4)
    blocks = blocks.reshape(n_rows, n_cols, ch_dev, tile_rows * tile_cols)
    tiles = to_tiles(blocks)
    mixed = prior_mix(tiles, gain, w_in, b_in, w_out)
    grid = mixed.reshape(-1, tile_rows, tile_cols)
    padded = padded_2(grid, (("rows", 1), ("cols", 2)), 1)
    result = (
        tiles.reshape(grid.shape).astype(jnp.float32) + spread(padded, kernel, tile_rows, tile_cols)
    ).astype(jnp.bfloat16)
    returned = to_planes(result.reshape(n_rows, n_cols, ch_dev, tile_rows * tile_cols))
    returned = returned.reshape(n_rows, n_cols, ch_dev, tile_rows, tile_cols).transpose(
        2, 0, 3, 1, 4
    )
    return returned.reshape(ch_dev, img_len, img_len)


def solution(mesh):
    return jax.shard_map(
        local,
        mesh=mesh,
        in_specs=(
            P(("rows", "cols"), None, None),
            P(("rows", "cols"), None, None),
            P(("rows", "cols"), None, None),
            P(("rows", "cols")),
            P(),
            P(),
            P(),
            P(),
            P(),
        ),
        out_specs=P(("rows", "cols"), None, None),
        check_vma=False,
    )
```

profile of v0, /device:TPU:1, one launch (start us, length us, event | category | flops | bytes accessed | tf_op | source)
XLA Modules:
  0.0 461.2 jit_solution(14562911728202955735)
XLA Ops:
  0.0 330.7 %while.13 = (s32[]{:T(128)}, bf16[2,512,512]{1,2,0:T(8,128)(2,1)S(1)}, bf16[2,512,512]{2,1,0:T(8,128)(2,1)}, f32[2]{0:T(128)}, bf16[2,512,512]{2,1,0:T(8,128)(2,...) while((s32[]{:T(128)}, ...), condition=%wide.region_1.2_spmd.clone.clone.clone, body=%wide.region_0.1_spmd.clone.clone.clone.sunk | while | flops 13292273664 | bytes 103559376 | solution.py:113
  1.6 10.0 %convolution_convert_fusion.6 = bf16[512,1024]{1,0:T(8,128)(2,1)S(1)} fusion(bf16[1,512,512]{2,1,0:T(8,128)(2,1)S(1)} %get-tuple-element.316), kind=kOutput, calls=%fused_computation.40.clone.1 | convolution fusion | flops 545259520 | bytes 1572864 | tf_op jit(solution)/shard_map/while/body/eval_jaxpr/dot_general | solution.py:32
  11.6 12.6 %fusion.214 = f32[1024,1024]{1,0:T(8,128)S(1)} fusion(bf16[512,1024]{1,0:T(8,128)(2,1)S(1)} %convolution_convert_fusion.6), kind=kOutput, calls=%fused_computation.60.clone.1 | convolution fusion | flops 1081606144 | bytes 5242880 | tf_op jit(solution)/shard_map/while/body/eval_jaxpr/dot_general | solution.py:34
  24.2 10.0 %negate_convert_fusion.2 = bf16[512,1024]{1,0:T(8,128)(2,1)S(1)} fusion(bf16[1,512,512]{2,1,0:T(8,128)(2,1)S(1)} %get-tuple-element.316), kind=kOutput, calls=%fused_computation.34.clone.1 | convolution fusion | flops 545783808 | bytes 1572864 | tf_op jit(solution)/shard_map/while/body/eval_jaxpr/dot_general | solution.py:33
  34.3 13.8 %convolution_add_fusion.6 = f32[1024,1024]{1,0:T(8,128)S(1)} fusion(f32[1024,1024]{1,0:T(8,128)S(1)} %fusion.214, bf16[512,1024]{1,0:T(8,128)(2,1)S(1)} %negate_convert_fusion.2), kind=kOutput, calls=%fused_computation.15.clone.1 | convolution fusion | flops 1082654720 | bytes 9437184 | tf_op jit(solution)/shard_map/while/body/eval_jaxpr/dot_general | solution.py:34
  78.8 12.6 %fusion.216 = f32[1024,1024]{1,0:T(8,128)S(1)} fusion(bf16[512,1024]{1,0:T(8,128)(2,1)S(1)} %negate_convert_fusion.2), kind=kOutput, calls=%fused_computation.59.clone.1 | convolution fusion | flops 1081606144 | bytes 5242880 | tf_op jit(solution)/shard_map/while/body/eval_jaxpr/dot_general | solution.py:37
  91.4 11.6 %multiply_convert_fusion.6 = (bf16[1024,1024]{1,0:T(8,128)(2,1)S(1)}, bf16[1024,1024]{1,0:T(8,128)(2,1)S(1)}) fusion(f32[1024,1024]{1,0:T(8,128)S(1)} %convolution_add_fusion.5, f32[1024,1024]{1,0:T(8,128)S(1)} %convolution_add_fusion.6, f32[1024,1024]{1,0:T(8,128)S(1)} %convolution_subtract_fusion.4, f32[1024,1024]{1,0:T(8,128)S(1)} %fusion.216, ...), kind=kOutput, calls=%fused_computation.6.clone.1 | convolution fusion | flops 1093140480 | bytes 22020096 | tf_op jit(solution)/shard_map/while/body/eval_jaxpr/dot_general | solution.py:37
  112.0 10.5 %add_convert_fusion.clone.7 = bf16[1024,512]{1,0:T(8,128)(2,1)} fusion(f32[1024,512]{1,0:T(8,128)S(1)} %fusion.219, bf16[1024,1024]{1,0:T(8,128)(2,1)S(1)} %get-tuple-element.318, s32[512]{0:T(512)S(1)} %get-tuple-element.342), kind=kOutput, calls=%fused_computation.32.clone.clone.clone.2.clone.1 | convolution fusion | flops 1082654720 | bytes 5244928 | tf_op jit(solution)/shard_map/while/body/eval_jaxpr/dot_general | solution.py:56
  131.3 10.0 %subtract_convert_fusion.clone.7 = bf16[1024,512]{1,0:T(8,128)(2,1)S(1)} fusion(f32[1024,512]{1,0:T(8,128)S(1)} %fusion.217, bf16[1024,1024]{1,0:T(8,128)(2,1)S(1)} %get-tuple-element.318, s32[512]{0:T(512)S(1)} %get-tuple-element.342), kind=kOutput, calls=%fused_computation.33.clone.clone.clone.2.clone.1 | convolution fusion | flops 1082654720 | bytes 5244928 | tf_op jit(solution)/shard_map/while/body/eval_jaxpr/dot_general | solution.py:52
  141.3 9.6 %fusion.218 = f32[512,512]{1,0:T(8,128)} fusion(s32[512]{0:T(512)S(1)} %get-tuple-element.342, bf16[1024,512]{1,0:T(8,128)(2,1)S(1)} %subtract_convert_fusion.clone.7), kind=kOutput, calls=%fused_computation.61.clone.3 | convolution fusion | flops 544735232 | bytes 2099200 | tf_op jit(solution)/shard_map/while/body/eval_jaxpr/dot_general | solution.py:58
  152.1 10.4 %fusion.220 = bf16[2,512,512]{1,2,0:T(8,128)(2,1)S(1)} fusion(bf16[2,512,512]{1,2,0:T(8,128)(2,1)S(1)} %get-tuple-element.329, s32[]{:T(128)} %get-tuple-element.328, f32[512,512]{1,0:T(8,128)} %fusion.218, s32[512]{0:T(512)S(1)} %get-tuple-element.342, bf16[1,512,512]{1,2,0:T(8,128)(2,1)S(1)} %copy.81, bf16[1,512,512]{1,2,0:T(8,128)(2,1)S(1)} %copy.82, ...), kind=kOutput, calls=%fused_computation.51.clone.3 | convolution fusion | flops 546570240 | bytes 3672072 | tf_op jit(solution)/shard_map/while/body/eval_jaxpr/dot_general | solution.py:58
  164.2 10.0 %convolution_convert_fusion.6 = bf16[512,1024]{1,0:T(8,128)(2,1)S(1)} fusion(bf16[1,512,512]{2,1,0:T(8,128)(2,1)S(1)} %get-tuple-element.316), kind=kOutput, calls=%fused_computation.40.clone.1 | convolution fusion | flops 545259520 | bytes 1572864 | tf_op jit(solution)/shard_map/while/body/eval_jaxpr/dot_general | solution.py:32
  174.2 12.6 %fusion.214 = f32[1024,1024]{1,0:T(8,128)S(1)} fusion(bf16[512,1024]{1,0:T(8,128)(2,1)S(1)} %convolution_convert_fusion.6), kind=kOutput, calls=%fused_computation.60.clone.1 | convolution fusion | flops 1081606144 | bytes 5242880 | tf_op jit(solution)/shard_map/while/body/eval_jaxpr/dot_general | solution.py:34
  186.8 10.0 %negate_convert_fusion.2 = bf16[512,1024]{1,0:T(8,128)(2,1)S(1)} fusion(bf16[1,512,512]{2,1,0:T(8,128)(2,1)S(1)} %get-tuple-element.316), kind=kOutput, calls=%fused_computation.34.clone.1 | convolution fusion | flops 545783808 | bytes 1572864 | tf_op jit(solution)/shard_map/while/body/eval_jaxpr/dot_general | solution.py:33
  196.9 13.8 %convolution_add_fusion.6 = f32[1024,1024]{1,0:T(8,128)S(1)} fusion(f32[1024,1024]{1,0:T(8,128)S(1)} %fusion.214, bf16[512,1024]{1,0:T(8,128)(2,1)S(1)} %negate_convert_fusion.2), kind=kOutput, calls=%fused_computation.15.clone.1 | convolution fusion | flops 1082654720 | bytes 9437184 | tf_op jit(solution)/shard_map/while/body/eval_jaxpr/dot_general | solution.py:34
  241.0 12.6 %fusion.216 = f32[1024,1024]{1,0:T(8,128)S(1)} fusion(bf16[512,1024]{1,0:T(8,128)(2,1)S(1)} %negate_convert_fusion.2), kind=kOutput, calls=%fused_computation.59.clone.1 | convolution fusion | flops 1081606144 | bytes 5242880 | tf_op jit(solution)/shard_map/while/body/eval_jaxpr/dot_general | solution.py:37
  253.6 11.6 %multiply_convert_fusion.6 = (bf16[1024,1024]{1,0:T(8,128)(2,1)S(1)}, bf16[1024,1024]{1,0:T(8,128)(2,1)S(1)}) fusion(f32[1024,1024]{1,0:T(8,128)S(1)} %convolution_add_fusion.5, f32[1024,1024]{1,0:T(8,128)S(1)} %convolution_add_fusion.6, f32[1024,1024]{1,0:T(8,128)S(1)} %convolution_subtract_fusion.4, f32[1024,1024]{1,0:T(8,128)S(1)} %fusion.216, ...), kind=kOutput, calls=%fused_computation.6.clone.1 | convolution fusion | flops 1093140480 | bytes 22020096 | tf_op jit(solution)/shard_map/while/body/eval_jaxpr/dot_general | solution.py:37
  265.2 9.1 %fusion.219 = f32[1024,512]{1,0:T(8,128)S(1)} fusion(bf16[1024,1024]{1,0:T(8,128)(2,1)S(1)} %get-tuple-element.317, s32[512]{0:T(512)S(1)} %get-tuple-element.342), kind=kOutput, calls=%fused_computation.63.clone.1 | convolution fusion | flops 1081606144 | bytes 4196352 | tf_op jit(solution)/shard_map/while/body/eval_jaxpr/dot_general | solution.py:55
  274.3 10.5 %add_convert_fusion.clone.7 = bf16[1024,512]{1,0:T(8,128)(2,1)} fusion(f32[1024,512]{1,0:T(8,128)S(1)} %fusion.219, bf16[1024,1024]{1,0:T(8,128)(2,1)S(1)} %get-tuple-element.318, s32[512]{0:T(512)S(1)} %get-tuple-element.342), kind=kOutput, calls=%fused_computation.32.clone.clone.clone.2.clone.1 | convolution fusion | flops 1082654720 | bytes 5244928 | tf_op jit(solution)/shard_map/while/body/eval_jaxpr/dot_general | solution.py:56
  293.5 10.2 %subtract_convert_fusion.clone.7 = bf16[1024,512]{1,0:T(8,128)(2,1)S(1)} fusion(f32[1024,512]{1,0:T(8,128)S(1)} %fusion.217, bf16[1024,1024]{1,0:T(8,128)(2,1)S(1)} %get-tuple-element.318, s32[512]{0:T(512)S(1)} %get-tuple-element.342), kind=kOutput, calls=%fused_computation.33.clone.clone.clone.2.clone.1 | convolution fusion | flops 1082654720 | bytes 5244928 | tf_op jit(solution)/shard_map/while/body/eval_jaxpr/dot_general | solution.py:52
  303.7 9.6 %fusion.218 = f32[512,512]{1,0:T(8,128)} fusion(s32[512]{0:T(512)S(1)} %get-tuple-element.342, bf16[1024,512]{1,0:T(8,128)(2,1)S(1)} %subtract_convert_fusion.clone.7), kind=kOutput, calls=%fused_computation.61.clone.3 | convolution fusion | flops 544735232 | bytes 2099200 | tf_op jit(solution)/shard_map/while/body/eval_jaxpr/dot_general | solution.py:58
  314.5 10.4 %fusion.220 = bf16[2,512,512]{1,2,0:T(8,128)(2,1)S(1)} fusion(bf16[2,512,512]{1,2,0:T(8,128)(2,1)S(1)} %get-tuple-element.329, s32[]{:T(128)} %get-tuple-element.328, f32[512,512]{1,0:T(8,128)} %fusion.218, s32[512]{0:T(512)S(1)} %get-tuple-element.342, bf16[1,512,512]{1,2,0:T(8,128)(2,1)S(1)} %copy.81, bf16[1,512,512]{1,2,0:T(8,128)(2,1)S(1)} %copy.82, ...), kind=kOutput, calls=%fused_computation.51.clone.3 | convolution fusion | flops 546570240 | bytes 3672072 | tf_op jit(solution)/shard_map/while/body/eval_jaxpr/dot_general | solution.py:58
  342.4 30.2 %all_to_all.18 = bf16[128,2,2048]{2,1,0:T(2,128)(2,1)S(1)} all-to-all(bf16[128,2,2048]{2,1,0:T(2,128)(2,1)S(1)} %copy.65), channel_id=1, replica_groups=mesh['rows'=8,'cols'=16] {'rows','cols'}, dimensions={0} | all-to-all | bytes 2097152 | tf_op jit(solution)/shard_map/all_to_all | solution.py:84
  420.4 29.5 %all_to_all.19 = bf16[128,2,2048]{2,1,0:T(2,128)(2,1)S(1)} all-to-all(bf16[128,2,2048]{2,1,0:T(2,128)(2,1)S(1)} %all_to_all.14), channel_id=1, replica_groups=mesh['rows'=8,'cols'=16] {'rows','cols'}, dimensions={0} | all-to-all | bytes 2097152 | tf_op jit(solution)/shard_map/all_to_all | solution.py:92
  (79 shorter events, 162.9 us)
Async XLA Ops:
  0.0 375.2 %copy-start = (bf16[256,256]{1,0:T(8,128)(2,1)S(1)}, bf16[256,256]{1,0:T(8,128)(2,1)}, u32[]{:S(2)}) copy-start(bf16[256,256]{1,0:T(8,128)(2,1)} %param.18) | copy-start | bytes 393220
  34.3 13.8 %copy-start.3 = (bf16[2,256,256]{2,1,0:T(8,128)(2,1)S(1)}, bf16[2,256,256]{2,1,0:T(8,128)(2,1)}, u32[]{:S(2)}) copy-start(bf16[2,256,256]{2,1,0:T(8,128)(2,1)} %get-tuple-element.341) | copy-start | bytes 786436 | tf_op jit(solution)/shard_map/while
  150.8 0.7 copy-start.7
  196.9 13.8 %copy-start.3 = (bf16[2,256,256]{2,1,0:T(8,128)(2,1)S(1)}, bf16[2,256,256]{2,1,0:T(8,128)(2,1)}, u32[]{:S(2)}) copy-start(bf16[2,256,256]{2,1,0:T(8,128)(2,1)} %get-tuple-element.341) | copy-start | bytes 786436 | tf_op jit(solution)/shard_map/while
  313.3 0.7 copy-start.7
  372.6 2.7 copy-start.4
  372.6 2.7 copy-start.5
  372.6 2.7 copy-start.6
  375.3 15.8 %copy-start.2 = (f32[3,3,256]{2,1,0:T(4,128)S(1)}, f32[3,3,256]{2,1,0:T(4,128)}, u32[]{:S(2)}) copy-start(f32[3,3,256]{2,1,0:T(4,128)} %param.19) | copy-start | bytes 27652
  378.1 2.6 collective-permute-start
  379.4 4.5 collective-permute-start.1
  384.0 18.9 %collective-permute-start.2 = (bf16[256,66,1]{0,1,2:T(8,128)(2,1)S(1)}, bf16[256,66,1]{0,1,2:T(8,128)(2,1)S(1)}, u32[]{:S(2)}, u32[]{:S(2)}) collective-permute-start(bf16[256,66,1]{0,1,2:T(8,128)(2,1)S(1)} %copy.77), channel_id=1, source_target_pairs={{0,1},{1,2},{2,3},{3,4},{4,5},{5,6},{6,7},{7,8},{8,9},{9,10},{10,1... | collective-permute-start | bytes 101384 | tf_op jit(solution)/shard_map/ppermute | solution.py:16
  389.1 13.9 %collective-permute-start.3 = (bf16[256,66,1]{0,1,2:T(8,128)(2,1)S(1)}, bf16[256,66,1]{0,1,2:T(8,128)(2,1)S(1)}, u32[]{:S(2)}, u32[]{:S(2)}) collective-permute-start(bf16[256,66,1]{0,1,2:T(8,128)(2,1)S(1)} %copy.78), channel_id=1, source_target_pairs={{1,0},{2,1},{3,2},{4,3},{5,4},{6,5},{7,6},{8,7},{9,8},{10,9},{11,1... | collective-permute-start | bytes 101384 | tf_op jit(solution)/shard_map/ppermute | solution.py:19
  402.9 1.6 copy-start.1
where the time goes:
time: 463 us; the launch traced here: 461 us
  matrix products  322 us (70%)
  blocking collectives  59.7 us (13%)
  local copies, waits for them, and re-layouts  54.9 us (12%)
  starting transfers between devices  9.56 us (2%)
  loops' own time  6.72 us (1%)
  other arithmetic  5 us (1%)
    dot_general x4, matrix products, spectrum(): jnp.dot(imag_a, sin_t.T, preferred_element_type=jnp.float32)  39.1 us
    dot_general x4, matrix products, spectrum(): jnp.dot(imag_a, cos_t.T, preferred_element_type=jnp.float32)  35.5 us
    dot_general x4, matrix products, spectrum(): jnp.dot(real_a, cos_t.T, preferred_element_type=jnp.float32)  35.4 us
    dot_general x4, matrix products, spectrum(): jnp.dot(real_a, sin_t.T, preferred_element_type=jnp.float32)  33.9 us
    all_to_all x1, blocking collectives, to_tiles(): lax.all_to_all(blocks.reshape(-1, pixels), ('rows', 'cols'), split_axis=0...  30.2 us
    all_to_all x1, blocking collectives, to_planes(): lax.all_to_all(blocks.reshape(-1, shape[3]), ('rows', 'cols'), split_axis...  29.5 us
    dot_general x4, matrix products, spectrum(): jnp.dot(sin_t, plane, preferred_element_type=jnp.float32)  29.2 us
    dot_general x4, matrix products, spectrum(): jnp.dot(cos_t, plane, preferred_element_type=jnp.float32)  29.1 us
  transfers between devices with their start and end apart: 4, of which 1 were waited for; matrix products, arithmetic and copies ran while one was open for 3% of the time, Pallas kernels for 0%

commit v1 on v0

v1 whole, which is shorter than its diff:
```python
import functools
import math

import jax
import jax.numpy as jnp
import ml_dtypes
import numpy as np
from jax import lax
from jax.experimental import pallas as pl
from jax.experimental.pallas import tpu as pltpu
from jax.sharding import PartitionSpec as P

BF16 = jnp.bfloat16
F32 = jnp.float32
IMG = 512
PSF = 256
LEN = IMG + PSF // 2
HALF = LEN // 2
TILE = 16
LANES = 128
STEP_COLS = 128


def angle(freq, place):
    turns = (2.0 * freq[:, None]) * place[None, :]
    return np.mod(turns, 2 * LEN) * (math.pi / LEN)


def make_tables():
    odd = np.arange(HALF) + 0.5
    even = np.arange(LEN).astype(np.float64)
    place = np.arange(IMG).astype(np.float64)
    window = place + PSF // 2
    first = angle(odd, place)
    rows_in = np.concatenate([np.cos(first), -np.sin(first)], axis=0)
    second = angle(even, place).T
    parts = []
    for start in range(0, LEN, STEP_COLS):
        cos = np.cos(second[:, start : start + STEP_COLS])
        sin = np.sin(second[:, start : start + STEP_COLS])
        parts.append(
            np.concatenate(
                [np.concatenate([cos, -sin], axis=1), np.concatenate([sin, cos], axis=1)], axis=0
            )
        )
    cols_in = np.stack(parts)
    back = angle(even, window)
    parts = []
    for start in range(0, LEN, STEP_COLS):
        cos = np.cos(back[start : start + STEP_COLS])
        sin = np.sin(back[start : start + STEP_COLS])
        parts.append(np.concatenate([cos, sin], axis=1))
        parts.append(np.concatenate([-sin, cos], axis=1))
    cols_out = np.concatenate(parts, axis=0)
    cols_out = np.stack(np.split(cols_out, 4, axis=1))
    last = angle(odd, window).T
    rows_out = np.concatenate([2 * np.cos(last), -2 * np.sin(last)], axis=1)
    swap = np.zeros((256, 256))
    index = np.arange(256)
    swap[index, (index % 16) * 16 + index // 16] = 1
    return [x.astype(ml_dtypes.bfloat16) for x in (rows_in, cols_in, cols_out, rows_out, swap)]


def dot(a, b):
    return jnp.dot(a, b, preferred_element_type=F32)


def deconvolve(plane, dirty, psf, rate, rows_in, cols_in, cols_out, rows_out, stepped, work):
    image, point, prod, back = work
    count = LEN // STEP_COLS
    low = dot(rows_in[...], plane[...]).astype(BF16)
    image[:, :IMG] = low[:HALF]
    image[:, IMG:] = low[HALF:]
    low = dot(rows_in[:, :PSF], psf[...]).astype(BF16)
    point[:, :PSF] = low[:HALF]
    point[:, PSF:] = low[HALF:]

    def columns(step, carry):
        tab = cols_in.at[step]
        x = dot(image[...], tab[...])
        q = dot(point[:, :PSF], tab[:PSF]) + dot(point[:, PSF:], tab[IMG : IMG + PSF])
        x = x * (1.0 / (LEN * LEN))
        real_x, imag_x = x[:, :STEP_COLS], x[:, STEP_COLS:]
        real_q, imag_q = q[:, :STEP_COLS], q[:, STEP_COLS:]
        prod[step, :, :STEP_COLS] = (real_x * real_q - imag_x * imag_q).astype(BF16)
        prod[step, :, STEP_COLS:] = (real_x * imag_q + imag_x * real_q).astype(BF16)
        return carry

    lax.fori_loop(0, count, columns, 0)
    for part in range(4):
        tab = cols_out.at[part]
        total = dot(prod[0], tab[: 2 * STEP_COLS])
        for step in range(1, count):
            total += dot(prod[step], tab[2 * STEP_COLS * step : 2 * STEP_COLS * (step + 1)])
        row, col = divmod(part, 2)
        back[row * HALF : (row + 1) * HALF, col * 256 : (col + 1) * 256] = total.astype(BF16)

    def rows(step, carry):
        at = pl.ds(pl.multiple_of(step * 128, 128), 128)
        blurred = dot(rows_out[at, :], back[...])
        held = plane[at, :].astype(F32)
        stepped[at, :] = (held + rate * (dirty[at, :].astype(F32) - blurred)).astype(BF16)
        return carry

    lax.fori_loop(0, IMG // 128, rows, 0)


def mix(tiles, gain, w_in, b_in, w_out, swap, mixed, work):
    normed, turned = work

    def power_of(group, total):
        at = pl.ds(pl.multiple_of(group * 256, 256), 256)
        v = tiles[at, :].astype(F32)
        v = v * v
        return total + jnp.sum(v.reshape(16, TILE, LANES), axis=0)

    power = lax.fori_loop(0, 16, power_of, jnp.zeros((TILE, LANES), F32))
    scale = lax.rsqrt(power * (1.0 / 256) + 1e-06)

    def turn(pair, carry):
        for side in range(2):
            group = pair * 2 + side
            for k in range(16):
                channel = group * 16 + k
                v = tiles[pl.ds(pl.multiple_of(channel * TILE, TILE), TILE), :].astype(F32)
                normed[k * 16 : (k + 1) * 16, side * LANES : (side + 1) * LANES] = (
                    v * scale * gain[channel]
                ).astype(BF16)
        moved = dot(swap[...], normed[...]).astype(BF16)
        for side in range(2):
            at = pl.ds(pl.multiple_of((pair * 2 + side) * 16, 16), 16)
            for r in range(TILE):
                turned[r // 2, at, (r % 2) * LANES : (r % 2 + 1) * LANES] = moved[
                    r * 16 : (r + 1) * 16, side * LANES : (side + 1) * LANES
                ]
        return carry

    lax.fori_loop(0, 8, turn, 0)
    w_in_t = w_in[...].astype(F32).T.astype(BF16)
    w_out_t = w_out[...].astype(F32).T.astype(BF16)
    bias = b_in[...]

    def layers(pair, carry):
        inner = dot(w_in_t, turned[pair]) + bias
        hidden = jax.nn.gelu(inner, approximate=True).astype(BF16)
        turned[pair] = dot(w_out_t, hidden).astype(BF16)
        return carry

    lax.fori_loop(0, TILE // 2, layers, 0)

    def turn_back(pair, carry):
        for side in range(2):
            at = pl.ds(pl.multiple_of((pair * 2 + side) * 16, 16), 16)
            for r in range(TILE):
                normed[r * 16 : (r + 1) * 16, side * LANES : (side + 1) * LANES] = turned[
                    r // 2, at, (r % 2) * LANES : (r % 2 + 1) * LANES
                ]
        moved = dot(swap[...], normed[...]).astype(BF16)
        for side in range(2):
            at = pl.ds(pl.multiple_of((pair * 2 + side) * 256, 256), 256)
            mixed[at, :] = moved[:, side * LANES : (side + 1) * LANES]
        return carry

    lax.fori_loop(0, 8, turn_back, 0)


def filter_plane(mixed, stepped, taps, out, wide):
    zero = jnp.zeros((8, IMG), F32)
    wide[:8] = zero
    wide[8 + IMG :] = zero

    def widen(step, carry):
        at = pl.multiple_of(step * 64, 64)
        wide[pl.ds(at + 8, 64), :] = mixed[pl.ds(at, 64), :].astype(F32)
        return carry

    lax.fori_loop(0, IMG // 64, widen, 0)
    rows = 32
    lane = lax.broadcasted_iota(jnp.int32, (rows, IMG), 1)

    def block(step, carry):
        at = pl.multiple_of(step * rows, rows)
        span = wide[pl.ds(at, rows + 16), :]
        lines = [span[7 + a : 7 + a + rows] for a in range(3)]
        sums = [sum(taps(a, b) * lines[a] for a in range(3)) for b in range(3)]
        left = jnp.where(lane == 0, 0.0, pltpu.roll(sums[0], 1, 1))
        right = jnp.where(lane == IMG - 1, 0.0, pltpu.roll(sums[2], IMG - 1, 1))
        total = stepped[pl.ds(at, rows), :].astype(F32) + (sums[1] + (left + right))
        out[pl.ds(at, rows), :] = total.astype(BF16)
        return carry

    lax.fori_loop(0, IMG // rows, block, 0)


def step_kernel(rate, model, dirty, psf, rows_in, cols_in, cols_out, rows_out, out, *work):
    for channel in range(2):
        deconvolve(
            model.at[channel], dirty.at[channel], psf.at[channel], rate[channel],
            rows_in, cols_in, cols_out, rows_out, out.at[channel], work,
        )


def mix_kernel(gain, tiles, w_in, b_in, w_out, swap, out, *work):
    mix(tiles, gain, w_in, b_in, w_out, swap, out, work)


def filter_kernel(taps, mixed, stepped, out, wide):
    for channel in range(2):
        filter_plane(
            mixed.at[channel], stepped.at[channel],
            lambda a, b: taps[channel * 9 + a * 3 + b], out.at[channel], wide,
        )


def local(model, dirty, psf, step_size, gain, w_in, b_in, w_out, kernel):
    rows_in, cols_in, cols_out, rows_out, swap = make_tables()
    smem = pl.BlockSpec(memory_space=pltpu.SMEM)
    vmem = pl.BlockSpec(memory_space=pltpu.VMEM)
    params = pltpu.CompilerParams(vmem_limit_bytes=56 << 20)
    stepped = pl.pallas_call(
        step_kernel,
        out_shape=jax.ShapeDtypeStruct((2, IMG, IMG), BF16),
        in_specs=[smem] + [vmem] * 7,
        out_specs=vmem,
        scratch_shapes=[
            pltpu.VMEM((HALF, 2 * IMG), BF16),
            pltpu.VMEM((HALF, 2 * PSF), BF16),
            pltpu.VMEM((LEN // STEP_COLS, HALF, 2 * STEP_COLS), BF16),
            pltpu.VMEM((LEN, IMG), BF16),
        ],
        compiler_params=params,
    )(step_size, model, dirty, psf, rows_in, cols_in, cols_out, rows_out)

    blocks = stepped.reshape(2, 32, TILE, 4, LANES).transpose(1, 3, 0, 2, 4)
    blocks = blocks.reshape(128, 2, TILE, LANES)
    tiles = lax.all_to_all(blocks, ("rows", "cols"), split_axis=0, concat_axis=0, tiled=True)
    mixed = pl.pallas_call(
        mix_kernel,
        out_shape=jax.ShapeDtypeStruct((256 * TILE, LANES), BF16),
        in_specs=[smem] + [vmem] * 5,
        out_specs=vmem,
        scratch_shapes=[pltpu.VMEM((256, 256), BF16), pltpu.VMEM((TILE // 2, 256, 256), BF16)],
        compiler_params=params,
    )(gain, tiles.reshape(256 * TILE, LANES), w_in, b_in[:, None], w_out, swap)
    back = lax.all_to_all(
        mixed.reshape(128, 2, TILE, LANES), ("rows", "cols"), split_axis=0, concat_axis=0, tiled=True
    )
    planes = back.reshape(32, 4, 2, TILE, LANES).transpose(2, 0, 3, 1, 4).reshape(2, IMG, IMG)
    me = lax.axis_index(("rows", "cols"))
    taps = lax.dynamic_slice_in_dim(kernel.reshape(9, 256), 2 * me, 2, axis=1).T.reshape(18)
    return pl.pallas_call(
        filter_kernel,
        out_shape=jax.ShapeDtypeStruct((2, IMG, IMG), BF16),
        in_specs=[smem] + [vmem] * 2,
        out_specs=vmem,
        scratch_shapes=[pltpu.VMEM((IMG + 16, IMG), F32)],
        compiler_params=params,
    )(taps, planes, stepped)


def solution(mesh):
    split = P(("rows", "cols"), None, None)
    return jax.shard_map(
        local,
        mesh=mesh,
        in_specs=(split, split, split, P(("rows", "cols")), P(), P(), P(), P(), P()),
        out_specs=split,
        check_vma=False,
    )
```

time: 463 us -> 91.1 us (0.20)
  matrix products: 322 us -> 0 us
  blocking collectives: 59.7 us -> 0 us
  local copies, waits for them, and re-layouts: 54.9 us -> 6.94 us
  waiting for transfers between devices: 3.18 us -> 36.2 us
  Pallas kernels: 0 us -> 31.2 us
  starting transfers between devices: 9.56 us -> 16.3 us
  loops' own time: 6.72 us -> 0 us
  other arithmetic: 5 us -> 0 us
    dot_general x37 -> x0, matrix products: 322 us -> none  [the longest x4 39.1 us: spectrum(): jnp.dot(imag_a, sin_t.T, preferred_element_type=jnp.float32)]
    all_to_all x2 -> x0, blocking collectives: 59.7 us -> none  [the longest x1 30.2 us: to_tiles(): lax.all_to_all(blocks.reshape(-1, pixels), ('rows', 'cols'), split_axis=0...]
    all_to_all x0 -> x2, waiting for transfers between devices: none -> 36.2 us  [the longest x1 18.1 us: local(): lax.all_to_all(blocks, ('rows', 'cols'), split_axis=0, concat_axis=0, til...]
    pallas_call x0 -> x3, Pallas kernels: none -> 31.2 us  [the longest x1 14.3 us: local(): pl.pallas_call(step_kernel, out_shape=jax.ShapeDtypeStruct((2, IMG, IMG),...]
    convert_element_type x4 -> x0, local copies, waits for them, and re-layouts: 19.8 us -> none  [the longest x2 11.8 us: local(): tiles.reshape(grid.shape).astype(jnp.float32)]
    all_to_all x0 -> x2, starting transfers between devices: none -> 16.3 us  [the longest x1 11.5 us: local(): lax.all_to_all(blocks, ('rows', 'cols'), split_axis=0, concat_axis=0, til...]
    all_to_all x4 -> x0, local copies, waits for them, and re-layouts: 14 us -> none  [the longest x2 7.08 us: to_tiles(): lax.all_to_all(blocks.reshape(-1, pixels), ('rows', 'cols'), split_axis=0...]
    ppermute x4 -> x0, starting transfers between devices: 9.56 us -> none  [the longest x2 6.34 us: padded_2(): lax.ppermute(lax.slice_in_dim(block, block.shape[dim] - width, None, axis...]
  transfers between devices with their start and end apart: 4 -> 2, of which waited for: 1 -> 2; matrix products, arithmetic and copies ran while one was open for 3% -> 2% of each run, Pallas kernels for 0% -> 0%
where the time goes in v1:
time: 91.1 us; the launch traced here: 90.8 us
  waiting for transfers between devices  36.2 us (40%)
  Pallas kernels  31.2 us (34%)
  starting transfers between devices  16.3 us (18%)
  local copies, waits for them, and re-layouts  6.94 us (8%)
    all_to_all x1, waiting for transfers between devices, local(): lax.all_to_all(blocks, ('rows', 'cols'), split_axis=0, concat_axis=0, til...  18.1 us
    all_to_all x1, waiting for transfers between devices, local(): lax.all_to_all(mixed.reshape(128, 2, TILE, LANES), ('rows', 'cols'), spli...  18.1 us
    pallas_call x1, Pallas kernels, local(): pl.pallas_call(step_kernel, out_shape=jax.ShapeDtypeStruct((2, IMG, IMG),...  14.3 us
    all_to_all x1, starting transfers between devices, local(): lax.all_to_all(blocks, ('rows', 'cols'), split_axis=0, concat_axis=0, til...  11.5 us
    pallas_call x1, Pallas kernels, local(): pl.pallas_call(mix_kernel, out_shape=jax.ShapeDtypeStruct((256 * TILE, LA...  9.87 us
    pallas_call x1, Pallas kernels, local(): pl.pallas_call(filter_kernel, out_shape=jax.ShapeDtypeStruct((2, IMG, IMG...  7.11 us
    all_to_all x1, starting transfers between devices, local(): lax.all_to_all(mixed.reshape(128, 2, TILE, LANES), ('rows', 'cols'), spli...  4.85 us
  transfers between devices with their start and end apart: 2, of which 2 were waited for; matrix products, arithmetic and copies ran while one was open for 2% of the time, Pallas kernels for 0%

profile of v1, /device:TPU:1, one launch (start us, length us, event | category | flops | bytes accessed | tf_op | source)
XLA Modules:
  0.0 90.8 jit_solution(380144167110825902)
XLA Ops:
  0.0 14.3 %shard_map.136.stepped = bf16[2,512,512]{2,1,0:T(8,128)(2,1)} custom-call(f32[2]{0:T(128)} %rate.1, bf16[2,512,512]{2,1,0:T(8,128)(2,1)} %model.1, bf16[2,512,512]{2,1,0:T(8,128)(2,1)} %dirty.1, bf16[2,256,256]{2,1,0:T(8,128)(2,1)} %psf.1, bf16[640,512]{1,0:T(8,128)(2,1)} %constant.27.clone.rows_in, bf16[5,1024,256]{2,1,0:T(8,128)(2,1)} %constant.28.clone.cols_in, ...), custom_call_target="tpu_custom_call" | custom-call | tf_op jit(solution)/shard_map/pallas_call | solution.py:220
  14.3 1.3 %reshape.26 = bf16[2,32,16,4,128]{4,3,2,1,0:T(4,128)(2,1)S(1)} reshape(bf16[2,512,512]{2,1,0:T(8,128)(2,1)} %shard_map.136.stepped) | data formatting | bytes 2097152 | tf_op jit(solution)/shard_map/reshape | solution.py:234
  15.6 0.0 copy-start.2
  15.6 1.2 %copy.18 = bf16[32,4,2,16,128]{4,3,2,1,0:T(8,128)(2,1)} copy(bf16[32,4,2,16,128]{4,1,3,0,2:T(4,128)(2,1)S(1)} %bitcast.12) | data formatting | bytes 2097152 | tf_op jit(solution)/shard_map/transpose | solution.py:234
  16.8 11.5 %all-to-all-start = ((bf16[128,2,16,128]{3,2,1,0:T(8,128)(2,1)}), bf16[128,2,16,128]{3,2,1,0:T(8,128)(2,1)S(1)}, u32[]{:S(2)}, u32[]{:S(2)}) async-start(bf16[128,2,16,128]{3,2,1,0:T(8,128)(2,1)} %bitcast.2), calls=%async_computation | async-start | bytes 2097152 | tf_op jit(solution)/shard_map/all_to_all | solution.py:236
  28.3 0.0 copy-start.1
  28.3 0.0 copy-done.2
  28.3 0.8 copy.19.b_in
  29.1 18.1 %all-to-all-done = bf16[128,2,16,128]{3,2,1,0:T(8,128)(2,1)S(1)} async-done(((bf16[128,2,16,128]{3,2,1,0:T(8,128)(2,1)}), bf16[128,2,16,128]{3,2,1,0:T(8,128)(2,1)S(1)}, u32[]{:S(2)}, u32[]{:S(2)}) %all-to-all-start) | async-done | bytes 1048608 | tf_op jit(solution)/shard_map/all_to_all | solution.py:236
  47.2 0.0 copy-start
  47.2 1.0 %copy-done = bf16[128,2,16,128]{3,2,1,0:T(8,128)(2,1)} copy-done((bf16[128,2,16,128]{3,2,1,0:T(8,128)(2,1)}, bf16[128,2,16,128]{3,2,1,0:T(8,128)(2,1)S(1)}, u32[]{:S(2)}) %copy-start) | copy-done | bytes 1048600
  48.2 9.9 %shard_map.137 = bf16[4096,128]{1,0:T(8,128)(2,1)} custom-call(f32[256]{0:T(256)} %gain.1, bf16[4096,128]{1,0:T(8,128)(2,1)} %bitcast.10, bf16[256,256]{1,0:T(8,128)(2,1)} %w_in.1, f32[256,1]{1,0:T(8,128)} %copy.19.b_in, bf16[256,256]{1,0:T(8,128)(2,1)} %w_out.1, bf16[256,256]{1,0:T(8,128)(2,1)} %constant.31.clone.swap), custom_call_target="tpu_custom_call" | custom-call | tf_op jit(solution)/shard_map/pallas_call | solution.py:237
  58.1 4.8 %all-to-all-start.1 = ((bf16[128,2,16,128]{3,2,1,0:T(8,128)(2,1)}), bf16[128,2,16,128]{3,2,1,0:T(8,128)(2,1)S(1)}, u32[]{:S(2)}, u32[]{:S(2)}) async-start(bf16[128,2,16,128]{3,2,1,0:T(8,128)(2,1)} %bitcast.9), calls=%async_computation.1 | async-start | bytes 2097152 | tf_op jit(solution)/shard_map/all_to_all | solution.py:245
  62.9 0.0 copy-done.1
  63.0 0.1 constant_dynamic-slice_fusion
  63.0 0.1 copy.21
  63.1 0.7 reshape.25.taps
  63.8 18.1 %all-to-all-done.1 = bf16[128,2,16,128]{3,2,1,0:T(8,128)(2,1)S(1)} async-done(((bf16[128,2,16,128]{3,2,1,0:T(8,128)(2,1)}), bf16[128,2,16,128]{3,2,1,0:T(8,128)(2,1)S(1)}, u32[]{:S(2)}, u32[]{:S(2)}) %all-to-all-start.1) | async-done | bytes 1048608 | tf_op jit(solution)/shard_map/all_to_all | solution.py:245
  81.9 0.5 copy.20
  82.4 1.3 %reshape.31.mixed = bf16[2,512,512]{2,1,0:T(8,128)(2,1)} reshape(bf16[2,32,16,4,128]{4,3,2,1,0:T(4,128)(2,1)S(1)} %copy.20) | data formatting | bytes 2097152 | tf_op jit(solution)/shard_map/reshape | solution.py:248
  83.7 7.1 %shard_map.138 = bf16[2,512,512]{2,1,0:T(8,128)(2,1)} custom-call(f32[18]{0:T(128)} %reshape.25.taps, bf16[2,512,512]{2,1,0:T(8,128)(2,1)} %reshape.31.mixed, bf16[2,512,512]{2,1,0:T(8,128)(2,1)} %shard_map.136.stepped), custom_call_target="tpu_custom_call" | custom-call | tf_op jit(solution)/shard_map/pallas_call | solution.py:251
  (1 shorter events, 0.0 us)
Async XLA Ops:
  15.6 12.7 %copy-start.2 = (f32[256]{0:T(256)S(1)}, f32[256]{0:T(256)}, u32[]{:S(2)}) copy-start(f32[256]{0:T(256)} %param.20) | copy-start | bytes 3076
  16.8 30.4 %all-to-all-start = ((bf16[128,2,16,128]{3,2,1,0:T(8,128)(2,1)}), bf16[128,2,16,128]{3,2,1,0:T(8,128)(2,1)S(1)}, u32[]{:S(2)}, u32[]{:S(2)}) async-start(bf16[128,2,16,128]{3,2,1,0:T(8,128)(2,1)} %bitcast.2), calls=%async_computation | async-start | bytes 2097152 | tf_op jit(solution)/shard_map/all_to_all | solution.py:236
  28.3 34.6 %copy-start.1 = (f32[3,3,256]{2,1,0:T(4,128)S(1)}, f32[3,3,256]{2,1,0:T(4,128)}, u32[]{:S(2)}) copy-start(f32[3,3,256]{2,1,0:T(4,128)} %param.22) | copy-start | bytes 27652
  47.2 1.0 %copy-start = (bf16[128,2,16,128]{3,2,1,0:T(8,128)(2,1)}, bf16[128,2,16,128]{3,2,1,0:T(8,128)(2,1)S(1)}, u32[]{:S(2)}) copy-start(bf16[128,2,16,128]{3,2,1,0:T(8,128)(2,1)S(1)} %all-to-all-done) | copy-start | bytes 3145732
  58.1 23.8 %all-to-all-start.1 = ((bf16[128,2,16,128]{3,2,1,0:T(8,128)(2,1)}), bf16[128,2,16,128]{3,2,1,0:T(8,128)(2,1)S(1)}, u32[]{:S(2)}, u32[]{:S(2)}) async-start(bf16[128,2,16,128]{3,2,1,0:T(8,128)(2,1)} %bitcast.9), calls=%async_computation.1 | async-start | bytes 2097152 | tf_op jit(solution)/shard_map/all_to_all | solution.py:245

commit v2 on v1

v2 whole, which is shorter than its diff:
```python
import math

import jax
import jax.numpy as jnp
import ml_dtypes
import numpy as np
from jax import lax
from jax.experimental import pallas as pl
from jax.experimental.pallas import tpu as pltpu
from jax.sharding import PartitionSpec as P

BF16 = jnp.bfloat16
F32 = jnp.float32
MESH = pl.DeviceIdType.MESH
IMG = 512
PSF = 256
LEN = IMG + PSF // 2
HALF = LEN // 2
TILE = 16
LANES = 128
CHIPS = 64
STEP_COLS = 128


def angle(freq, place):
    turns = (2.0 * freq[:, None]) * place[None, :]
    return np.mod(turns, 2 * LEN) * (math.pi / LEN)


def make_tables():
    odd = np.arange(HALF) + 0.5
    even = np.arange(LEN).astype(np.float64)
    place = np.arange(IMG).astype(np.float64)
    window = place + PSF // 2
    first = angle(odd, place)
    rows_in = np.concatenate([np.cos(first), -np.sin(first)], axis=0)
    second = angle(even, place).T
    parts = []
    for start in range(0, LEN, STEP_COLS):
        cos = np.cos(second[:, start : start + STEP_COLS])
        sin = np.sin(second[:, start : start + STEP_COLS])
        parts.append(
            np.concatenate(
                [np.concatenate([cos, -sin], axis=1), np.concatenate([sin, cos], axis=1)], axis=0
            )
        )
    cols_in = np.stack(parts)
    back = angle(even, window)
    parts = []
    for start in range(0, LEN, STEP_COLS):
        cos = np.cos(back[start : start + STEP_COLS])
        sin = np.sin(back[start : start + STEP_COLS])
        parts.append(np.concatenate([cos, sin], axis=1))
        parts.append(np.concatenate([-sin, cos], axis=1))
    cols_out = np.concatenate(parts, axis=0)
    cols_out = np.stack(np.split(cols_out, 4, axis=1))
    last = angle(odd, window).T
    rows_out = np.concatenate([2 * np.cos(last), -2 * np.sin(last)], axis=1)
    swap = np.zeros((256, 256))
    index = np.arange(256)
    swap[index, (index % 16) * 16 + index // 16] = 1
    order = np.zeros((256, 256))
    order[index, (index % 2) * 128 + index // 2] = 1
    tables = (rows_in, cols_in, cols_out, rows_out, swap, order)
    return [x.astype(ml_dtypes.bfloat16) for x in tables]


def dot(a, b):
    return jnp.dot(a, b, preferred_element_type=F32)


def copy_here(src, dst, sem):
    return pltpu.make_async_copy(src, dst, sem)


def first_axis(plane, psf, rows_in, image, point):
    low = dot(rows_in[...], plane[...]).astype(BF16)
    image[:, :IMG] = low[:HALF]
    image[:, IMG:] = low[HALF:]
    low = dot(rows_in[:, :PSF], psf[...]).astype(BF16)
    point[:, :PSF] = low[:HALF]
    point[:, PSF:] = low[HALF:]


def second_axis(cols_in, image, point, prod):
    def columns(step, carry):
        tab = cols_in.at[step]
        x = dot(image[...], tab[...])
        q = dot(point[:, :PSF], tab[:PSF]) + dot(point[:, PSF:], tab[IMG : IMG + PSF])
        x = x * (1.0 / (LEN * LEN))
        real_x, imag_x = x[:, :STEP_COLS], x[:, STEP_COLS:]
        real_q, imag_q = q[:, :STEP_COLS], q[:, STEP_COLS:]
        prod[step, :, :STEP_COLS] = (real_x * real_q - imag_x * imag_q).astype(BF16)
        prod[step, :, STEP_COLS:] = (real_x * imag_q + imag_x * real_q).astype(BF16)
        return carry

    lax.fori_loop(0, LEN // STEP_COLS, columns, 0)


def second_axis_back(cols_out, prod, back):
    for part in range(4):
        tab = cols_out.at[part]
        total = dot(prod[0], tab[: 2 * STEP_COLS])
        for step in range(1, LEN // STEP_COLS):
            total += dot(prod[step], tab[2 * STEP_COLS * step : 2 * STEP_COLS * (step + 1)])
        row, col = divmod(part, 2)
        back[row * HALF : (row + 1) * HALF, col * 256 : (col + 1) * 256] = total.astype(BF16)


def filter_plane(mixed, stepped, taps, out, wide):
    zero = jnp.zeros((8, IMG), F32)
    wide[:8] = zero
    wide[8 + IMG :] = zero

    def widen(step, carry):
        at = pl.multiple_of(step * 64, 64)
        wide[pl.ds(at + 8, 64), :] = mixed[pl.ds(at, 64), :].astype(F32)
        return carry

    lax.fori_loop(0, IMG // 64, widen, 0)
    rows = 32
    lane = lax.broadcasted_iota(jnp.int32, (rows, IMG), 1)

    def block(step, carry):
        at = pl.multiple_of(step * rows, rows)
        span = wide[pl.ds(at, rows + 16), :]
        lines = [span[7 + a : 7 + a + rows] for a in range(3)]
        sums = [sum(taps(a, b) * lines[a] for a in range(3)) for b in range(3)]
        left = jnp.where(lane == 0, 0.0, pltpu.roll(sums[0], 1, 1))
        right = jnp.where(lane == IMG - 1, 0.0, pltpu.roll(sums[2], IMG - 1, 1))
        total = stepped[pl.ds(at, rows), :].astype(F32) + (sums[1] + (left + right))
        out[pl.ds(at, rows), :] = total.astype(BF16)
        return carry

    lax.fori_loop(0, IMG // rows, block, 0)


def whole(
    rate, taps, model_h, dirty_h, psf_h, rows_in_h, cols_in_h, cols_out_h, rows_out_h,
    swap, order, gain, w_in, b_in, w_out, out_h,
    model, dirty, psf, rows_in, cols_in, cols_out, rows_out,
    image, point, prod, back, stepped, halves, parcel, tiles, turned, inner, scale,
    mixed, returned, planes, out, wide,
    load_sem, out_sem, pair_send, pair_recv, go_send, go_recv, ret_send, ret_recv, fin_send, fin_recv,
):
    row_at, col_at = lax.axis_index("rows"), lax.axis_index("cols")
    chip = row_at * 8 + col_at // 2
    core = col_at % 2
    sibling = {"rows": row_at, "cols": col_at + 1 - 2 * core}

    def at_chip(other):
        return {"rows": other // 8, "cols": (other % 8) * 2 + core}

    loads = []
    for src, dst in (
        (rows_in_h, rows_in),
        (model_h.at[0], model.at[0]),
        (psf_h, psf),
        (cols_in_h, cols_in),
        (cols_out_h, cols_out),
        (rows_out_h, rows_out),
        (dirty_h, dirty),
        (model_h.at[1], model.at[1]),
    ):
        copy = copy_here(src, dst, load_sem.at[len(loads)])
        copy.start()
        loads.append(copy)

    barrier = pltpu.get_barrier_semaphore()
    pl.semaphore_signal(barrier, inc=1, device_id=sibling, device_id_type=MESH)

    def greet(k, carry):
        pl.semaphore_signal(barrier, inc=1, device_id=at_chip(chip ^ k), device_id_type=MESH)
        return carry

    lax.fori_loop(1, CHIPS, greet, 0)

    def last_axis(channel):
        def rows(step, carry):
            at = pl.ds(pl.multiple_of(step * 128, 128), 128)
            blurred = dot(rows_out[at, :], back[...])
            held = model[channel, at, :].astype(F32)
            ahead = held + rate[channel] * (dirty[channel, at, :].astype(F32) - blurred)
            ahead = ahead.astype(BF16)
            stepped[channel, at, :] = ahead
            mine = jnp.where(core == 0, ahead[:, :256], ahead[:, 256:])
            other = jnp.where(core == 0, ahead[:, 256:], ahead[:, :256])
            halves[channel, core, at, :] = mine
            parcel[channel, at, :] = other
            return carry

        lax.fori_loop(0, IMG // 128, rows, 0)

    def pair_copy(channel):
        return pltpu.make_async_remote_copy(
            src_ref=parcel.at[channel],
            dst_ref=halves.at[channel, core],
            send_sem=pair_send.at[channel],
            recv_sem=pair_recv.at[channel],
            device_id=sibling,
            device_id_type=MESH,
        )

    def tile_of(planes_ref, other):
        at = pl.ds(pl.multiple_of((other // 2) * TILE, TILE), TILE)
        return planes_ref.at[:, at, pl.ds(pl.multiple_of((other % 2) * LANES, LANES), LANES)]

    def send_tiles(channel):
        def send(k, carry):
            other = chip ^ k
            pltpu.make_async_remote_copy(
                src_ref=tile_of(halves.at[channel], other),
                dst_ref=tiles.at[channel, pl.ds(chip * 2, 2)],
                send_sem=go_send.at[channel],
                recv_sem=go_recv.at[channel],
                device_id=at_chip(other),
                device_id_type=MESH,
            ).start()
            return carry

        lax.fori_loop(1, CHIPS, send, 0)
        copy_here(
            tile_of(halves.at[channel], chip),
            tiles.at[channel, pl.ds(chip * 2, 2)],
            go_recv.at[channel],
        ).start()

    def return_tiles(channel):
        def send(k, carry):
            other = chip ^ k
            pltpu.make_async_remote_copy(
                src_ref=mixed.at[channel, pl.ds(other * 2, 2)],
                dst_ref=tile_of(returned.at[channel], chip),
                send_sem=ret_send.at[channel],
                recv_sem=ret_recv.at[channel],
                device_id=at_chip(other),
                device_id_type=MESH,
            ).start()
            return carry

        lax.fori_loop(1, CHIPS, send, 0)
        copy_here(
            mixed.at[channel, pl.ds(chip * 2, 2)],
            tile_of(returned.at[channel], chip),
            ret_recv.at[channel],
        ).start()

    def half_at(which):
        return pl.ds(pl.multiple_of(which * 256, 256), 256)

    def final_copy(channel):
        return pltpu.make_async_remote_copy(
            src_ref=returned.at[channel, 1 - core],
            dst_ref=planes.at[channel, :, half_at(core)],
            send_sem=fin_send.at[channel],
            recv_sem=fin_recv.at[channel],
            device_id=sibling,
            device_id_type=MESH,
        )

    for load in loads[:3]:
        load.wait()
    first_axis(model.at[0], psf.at[0], rows_in, image, point)
    loads[3].wait()
    second_axis(cols_in, image, point, prod)
    loads[4].wait()
    second_axis_back(cols_out, prod, back)
    loads[5].wait()
    loads[6].wait()
    last_axis(0)
    pl.semaphore_wait(barrier, CHIPS)
    pair_copy(0).start()
    loads[7].wait()
    first_axis(model.at[1], psf.at[1], rows_in, image, point)
    pair_copy(0).wait_recv()
    send_tiles(0)
    second_axis(cols_in, image, point, prod)
    second_axis_back(cols_out, prod, back)
    last_axis(1)
    pair_copy(1).start()

    w_in_t = (w_in[...].astype(F32).T * gain[...]).astype(BF16)
    w_in_t = dot(w_in_t, order[...]).astype(BF16)
    w_out_t = dot(w_out[...], order[...]).T.astype(BF16)
    bias = jnp.broadcast_to(b_in[...], (LANES, 256)).T
    bias = jnp.concatenate([bias, bias], axis=1)

    pair_copy(1).wait_recv()
    send_tiles(1)

    def power_of(channel, total):
        def add(group, total):
            v = tiles[channel, pl.ds(pl.multiple_of(group * 16, 16), 16)].astype(F32)
            return total + jnp.sum(v * v, axis=0)

        return lax.fori_loop(0, 8, add, total)

    def turn(channel):
        def pairs(pair, carry):
            sides = [
                tiles[channel, pl.ds(pl.multiple_of(pair * 32 + side * 16, 16), 16)].reshape(256, LANES)
                for side in range(2)
            ]
            moved = dot(swap[...], jnp.concatenate(sides, axis=1)).astype(BF16)
            for side in range(2):
                at = pl.ds(pl.multiple_of(pair * 32 + side * 16, 16), 16)
                for r in range(TILE):
                    turned[channel, r // 2, at, (r % 2) * LANES : (r % 2 + 1) * LANES] = moved[
                        r * 16 : (r + 1) * 16, side * LANES : (side + 1) * LANES
                    ]
            return carry

        lax.fori_loop(0, 4, pairs, 0)

    def turn_back(channel):
        def pairs(pair, carry):
            sides = []
            for side in range(2):
                at = pl.ds(pl.multiple_of(pair * 32 + side * 16, 16), 16)
                lines = [
                    turned[channel, r // 2, at, (r % 2) * LANES : (r % 2 + 1) * LANES]
                    for r in range(TILE)
                ]
                sides.append(jnp.concatenate(lines, axis=0))
            moved = dot(swap[...], jnp.concatenate(sides, axis=1)).astype(BF16)
            for side in range(2):
                at = pl.ds(pl.multiple_of(pair * 32 + side * 16, 16), 16)
                mixed[channel, at] = moved[:, side * LANES : (side + 1) * LANES].reshape(16, TILE, LANES)
            return carry

        lax.fori_loop(0, 4, pairs, 0)

    copy_here(tiles.at[0], tiles.at[0], go_recv.at[0]).wait()
    power = power_of(0, jnp.zeros((TILE, LANES), F32))
    turn(0)

    def layer_part(pair, carry):
        inner[pair] = dot(w_in_t[:, :128], turned[0, pair])
        return carry

    lax.fori_loop(0, TILE // 2, layer_part, 0)
    copy_here(tiles.at[1], tiles.at[1], go_recv.at[1]).wait()
    power = power_of(1, power)
    scale[...] = lax.rsqrt(power * (1.0 / 256) + 1e-06)
    turn(1)

    def layers(pair, carry):
        factor = jnp.concatenate([scale[pl.ds(2 * pair, 1), :], scale[pl.ds(2 * pair + 1, 1), :]], axis=1)
        total = inner[pair] + dot(w_in_t[:, 128:], turned[1, pair])
        hidden = jax.nn.gelu(total * factor + bias, approximate=True).astype(BF16)
        result = dot(w_out_t, hidden).astype(BF16)
        turned[0, pair] = result[:128]
        turned[1, pair] = result[128:]
        return carry

    lax.fori_loop(0, TILE // 2, layers, 0)
    for channel in range(2):
        turn_back(channel)
        return_tiles(channel)

    for channel in range(2):
        copy_here(returned.at[channel], returned.at[channel], ret_recv.at[channel]).wait()
        final_copy(channel).start()
        planes[channel, :, half_at(core)] = returned[channel, core]
        final_copy(channel).wait_recv()
        filter_plane(
            planes.at[channel], stepped.at[channel],
            lambda a, b: taps[a, b, (chip * 2 + core) * 2 + channel], out.at[channel], wide,
        )
        copy_here(out.at[channel], out_h.at[channel], out_sem.at[channel]).start()
    for channel in range(2):
        pair_copy(channel).wait_send()
        final_copy(channel).wait_send()
        sent = tiles.at[channel, pl.ds(0, 2 * CHIPS - 2)]
        copy_here(sent, sent, go_send.at[channel]).wait()
        copy_here(sent, sent, ret_send.at[channel]).wait()
        copy_here(out.at[channel], out_h.at[channel], out_sem.at[channel]).wait()


def local(model, dirty, psf, step_size, gain, w_in, b_in, w_out, kernel):
    rows_in, cols_in, cols_out, rows_out, swap, order = make_tables()
    smem = pl.BlockSpec(memory_space=pltpu.SMEM)
    vmem = pl.BlockSpec(memory_space=pltpu.VMEM)
    hbm = pl.BlockSpec(memory_space=pl.ANY)
    dma = pltpu.SemaphoreType.DMA
    steps = LEN // STEP_COLS
    return pl.pallas_call(
        whole,
        out_shape=jax.ShapeDtypeStruct((2, IMG, IMG), BF16),
        in_specs=[smem] * 2 + [hbm] * 7 + [vmem] * 6,
        out_specs=hbm,
        scratch_shapes=[
            pltpu.VMEM((2, IMG, IMG), BF16),
            pltpu.VMEM((2, IMG, IMG), BF16),
            pltpu.VMEM((2, PSF, PSF), BF16),
            pltpu.VMEM(rows_in.shape, BF16),
            pltpu.VMEM(cols_in.shape, BF16),
            pltpu.VMEM(cols_out.shape, BF16),
            pltpu.VMEM(rows_out.shape, BF16),
            pltpu.VMEM((HALF, 2 * IMG), BF16),
            pltpu.VMEM((HALF, 2 * PSF), BF16),
            pltpu.VMEM((steps, HALF, 2 * STEP_COLS), BF16),
            pltpu.VMEM((LEN, IMG), BF16),
            pltpu.VMEM((2, IMG, IMG), BF16),
            pltpu.VMEM((2, 2, IMG, 256), BF16),
            pltpu.VMEM((2, IMG, 256), BF16),
            pltpu.VMEM((2, 128, TILE, LANES), BF16),
            pltpu.VMEM((2, TILE // 2, 128, 256), BF16),
            pltpu.VMEM((TILE // 2, 256, 256), F32),
            pltpu.VMEM((TILE, LANES), F32),
            pltpu.VMEM((2, 128, TILE, LANES), BF16),
            pltpu.VMEM((2, 2, IMG, 256), BF16),
            pltpu.VMEM((2, IMG, IMG), BF16),
            pltpu.VMEM((2, IMG, IMG), BF16),
            pltpu.VMEM((IMG + 16, IMG), F32),
            dma((8,)),
        ]
        + [dma((2,))] * 9,
        compiler_params=pltpu.CompilerParams(
            vmem_limit_bytes=64 << 20, collective_id=0, has_side_effects=True
        ),
    )(
        step_size, kernel, model, dirty, psf, rows_in, cols_in, cols_out, rows_out,
        swap, order, gain[None, :], w_in, b_in[None, :], w_out,
    )


def solution(mesh):
    split = P(("rows", "cols"), None, None)
    return jax.shard_map(
        local,
        mesh=mesh,
        in_specs=(split, split, split, P(("rows", "cols")), P(), P(), P(), P(), P()),
        out_specs=split,
        check_vma=False,
    )
```

time: 91.1 us -> 58.5 us (0.64)
  waiting for transfers between devices: 36.2 us -> 0 us
  Pallas kernels: 31.2 us -> 56.1 us
  starting transfers between devices: 16.3 us -> 0 us
  local copies, waits for them, and re-layouts: 6.94 us -> 2.26 us
    all_to_all x2 -> x0, waiting for transfers between devices: 36.2 us -> none  [the longest x1 18.1 us: local(): lax.all_to_all(blocks, ('rows', 'cols'), split_axis=0, concat_axis=0, til...]
    pallas_call x3 -> x1, Pallas kernels: 31.2 us -> 56.1 us  [local(): pl.pallas_call(whole, out_shape=jax.ShapeDtypeStruct((2, IMG, IMG), BF16)...]
    all_to_all x2 -> x0, starting transfers between devices: 16.3 us -> none  [the longest x1 11.5 us: local(): lax.all_to_all(blocks, ('rows', 'cols'), split_axis=0, concat_axis=0, til...]
    reshape x4 -> x0, local copies, waits for them, and re-layouts: 3.27 us -> none  [the longest x1 1.34 us: local(): blocks = stepped.reshape(2, 32, TILE, 4, LANES).transpose(1, 3, 0, 2, 4)]
    transpose x2 -> x0, local copies, waits for them, and re-layouts: 1.72 us -> none  [the longest x1 1.18 us: local(): blocks = stepped.reshape(2, 32, TILE, 4, LANES).transpose(1, 3, 0, 2, 4)]
    unnamed x7 -> x1, local copies, waits for them, and re-layouts: 1.08 us -> 2.26 us
  transfers between devices with their start and end apart: 2 -> 0, of which waited for: 2 -> 0; matrix products, arithmetic and copies ran while one was open for 2% -> 0% of each run, Pallas kernels for 0% -> 0%
where the time goes in v2:
time: 58.5 us; the launch traced here: 58.4 us
  Pallas kernels  56.1 us (96%)
  local copies, waits for them, and re-layouts  2.26 us (4%)
    pallas_call x1, Pallas kernels, local(): pl.pallas_call(whole, out_shape=jax.ShapeDtypeStruct((2, IMG, IMG), BF16)...  56.1 us
    unnamed x1, local copies, waits for them, and re-layouts  2.26 us

profile of v2, /device:TPU:1, one launch (start us, length us, event | category | flops | bytes accessed | tf_op | source)
XLA Modules:
  0.0 58.4 jit_solution(17519225100030536315)
XLA Ops:
  0.0 56.1 %shard_map.145 = bf16[2,512,512]{2,1,0:T(8,128)(2,1)} custom-call(f32[2]{0:T(128)} %rate.1, f32[3,3,256]{2,1,0:T(4,128)} %taps.1, bf16[2,512,512]{2,1,0:T(8,128)(2,1)} %model_h.1, bf16[2,512,512]{2,1,0:T(8,128)(2,1)} %dirty_h.1, bf16[2,256,256]{2,1,0:T(8,128)(2,1)} %psf_h.1, bf16[640,512]{1,0:T(8,128)(2,1)} %constant.12.clone.rows_in_h, ...), custom_call_target="tpu_custom_call" | custom-call | tf_op jit(solution)/shard_map/pallas_call | solution.py:387
  56.1 2.3 %copy.17 = bf16[2,512,512]{2,1,0:T(8,128)(2,1)} copy(bf16[2,512,512]{2,1,0:T(8,128)(2,1)} %shard_map.145) | data formatting | bytes 2097152

commit v3 on v2

--- a/solution.py
+++ b/solution.py
@@ -60,7 +60,7 @@
     index = np.arange(256)
     swap[index, (index % 16) * 16 + index // 16] = 1
     order = np.zeros((256, 256))
-    order[index, (index % 2) * 128 + index // 2] = 1
+    order[index, (index % 2) * 128 + (index // 2 % 2) * CHIPS + index // 4] = 1
     tables = (rows_in, cols_in, cols_out, rows_out, swap, order)
     return [x.astype(ml_dtypes.bfloat16) for x in tables]
 
@@ -94,7 +94,7 @@
         prod[step, :, STEP_COLS:] = (real_x * imag_q + imag_x * real_q).astype(BF16)
         return carry
 
-    lax.fori_loop(0, LEN // STEP_COLS, columns, 0)
+    lax.fori_loop(0, LEN // STEP_COLS, columns, 0, unroll=True)
 
 
 def second_axis_back(cols_out, prod, back):
@@ -117,7 +117,7 @@
         wide[pl.ds(at + 8, 64), :] = mixed[pl.ds(at, 64), :].astype(F32)
         return carry
 
-    lax.fori_loop(0, IMG // 64, widen, 0)
+    lax.fori_loop(0, IMG // 64, widen, 0, unroll=4)
     rows = 32
     lane = lax.broadcasted_iota(jnp.int32, (rows, IMG), 1)
 
@@ -132,15 +132,16 @@
         out[pl.ds(at, rows), :] = total.astype(BF16)
         return carry
 
-    lax.fori_loop(0, IMG // rows, block, 0)
+    lax.fori_loop(0, IMG // rows, block, 0, unroll=4)
 
 
 def whole(
-    rate, taps, model_h, dirty_h, psf_h, rows_in_h, cols_in_h, cols_out_h, rows_out_h,
-    swap, order, gain, w_in, b_in, w_out, out_h,
+    rate_h, taps_h, model_h, dirty_h, psf_h, rows_in_h, cols_in_h, cols_out_h, rows_out_h,
+    swap_h, order_h, gain_h, w_in_h, b_in_h, w_out_h, out_h,
+    rate, taps, swap, order, gain, w_in, b_in, w_out,
     model, dirty, psf, rows_in, cols_in, cols_out, rows_out,
     image, point, prod, back, stepped, halves, parcel, tiles, turned, inner, scale,
-    mixed, returned, planes, out, wide,
+    mixed, joined, planes, out, wide,
     load_sem, out_sem, pair_send, pair_recv, go_send, go_recv, ret_send, ret_recv, fin_send, fin_recv,
 ):
     row_at, col_at = lax.axis_index("rows"), lax.axis_index("cols")
@@ -161,6 +162,14 @@
         (rows_out_h, rows_out),
         (dirty_h, dirty),
         (model_h.at[1], model.at[1]),
+        (rate_h, rate),
+        (swap_h, swap),
+        (order_h, order),
+        (gain_h, gain),
+        (w_in_h, w_in),
+        (b_in_h, b_in),
+        (w_out_h, w_out),
+        (taps_h, taps),
     ):
         copy = copy_here(src, dst, load_sem.at[len(loads)])
         copy.start()
@@ -183,13 +192,13 @@
             ahead = held + rate[channel] * (dirty[channel, at, :].astype(F32) - blurred)
             ahead = ahead.astype(BF16)
             stepped[channel, at, :] = ahead
-            mine = jnp.where(core == 0, ahead[:, :256], ahead[:, 256:])
-            other = jnp.where(core == 0, ahead[:, 256:], ahead[:, :256])
-            halves[channel, core, at, :] = mine
-            parcel[channel, at, :] = other
+            first = jnp.concatenate([ahead[:, :128], ahead[:, 256:384]], axis=1)
+            second = jnp.concatenate([ahead[:, 128:256], ahead[:, 384:]], axis=1)
+            halves[channel, core, at, :] = jnp.where(core == 0, first, second)
+            parcel[channel, at, :] = jnp.where(core == 0, second, first)
             return carry
 
-        lax.fori_loop(0, IMG // 128, rows, 0)
+        lax.fori_loop(0, IMG // 128, rows, 0, unroll=True)
 
     def pair_copy(channel):
         return pltpu.make_async_remote_copy(
@@ -205,12 +214,18 @@
         at = pl.ds(pl.multiple_of((other // 2) * TILE, TILE), TILE)
         return planes_ref.at[:, at, pl.ds(pl.multiple_of((other % 2) * LANES, LANES), LANES)]
 
+    def place_of(plane_ref, other):
+        at = pl.ds(pl.multiple_of((other // 2) * TILE, TILE), TILE)
+        return plane_ref.at[at, pl.ds(pl.multiple_of((other % 2) * 256, 256), 256)]
+
+    core_lanes = pl.ds(pl.multiple_of(core * LANES, LANES), LANES)
+
     def send_tiles(channel):
         def send(k, carry):
             other = chip ^ k
             pltpu.make_async_remote_copy(
                 src_ref=tile_of(halves.at[channel], other),
-                dst_ref=tiles.at[channel, pl.ds(chip * 2, 2)],
+                dst_ref=tiles.at[channel, :, chip],
                 send_sem=go_send.at[channel],
                 recv_sem=go_recv.at[channel],
                 device_id=at_chip(other),
@@ -221,7 +236,7 @@
         lax.fori_loop(1, CHIPS, send, 0)
         copy_here(
             tile_of(halves.at[channel], chip),
-            tiles.at[channel, pl.ds(chip * 2, 2)],
+            tiles.at[channel, :, chip],
             go_recv.at[channel],
         ).start()
 
@@ -229,8 +244,8 @@
         def send(k, carry):
             other = chip ^ k
             pltpu.make_async_remote_copy(
-                src_ref=mixed.at[channel, pl.ds(other * 2, 2)],
-                dst_ref=tile_of(returned.at[channel], chip),
+                src_ref=joined.at[channel, other],
+                dst_ref=place_of(planes.at[channel], chip),
                 send_sem=ret_send.at[channel],
                 recv_sem=ret_recv.at[channel],
                 device_id=at_chip(other),
@@ -240,18 +255,15 @@
 
         lax.fori_loop(1, CHIPS, send, 0)
         copy_here(
-            mixed.at[channel, pl.ds(chip * 2, 2)],
-            tile_of(returned.at[channel], chip),
+            joined.at[channel, chip],
+            place_of(planes.at[channel], chip),
             ret_recv.at[channel],
         ).start()
 
-    def half_at(which):
-        return pl.ds(pl.multiple_of(which * 256, 256), 256)
-
-    def final_copy(channel):
+    def swap_mixed(channel):
         return pltpu.make_async_remote_copy(
-            src_ref=returned.at[channel, 1 - core],
-            dst_ref=planes.at[channel, :, half_at(core)],
+            src_ref=mixed.at[channel],
+            dst_ref=joined.at[channel, :, :, core_lanes],
             send_sem=fin_send.at[channel],
             recv_sem=fin_recv.at[channel],
             device_id=sibling,
@@ -267,6 +279,7 @@
     second_axis_back(cols_out, prod, back)
     loads[5].wait()
     loads[6].wait()
+    loads[8].wait()
     last_axis(0)
     pl.semaphore_wait(barrier, CHIPS)
     pair_copy(0).start()
@@ -279,6 +292,8 @@
     last_axis(1)
     pair_copy(1).start()
 
+    for load in loads[9:]:
+        load.wait()
     w_in_t = (w_in[...].astype(F32).T * gain[...]).astype(BF16)
     w_in_t = dot(w_in_t, order[...]).astype(BF16)
     w_out_t = dot(w_out[...], order[...]).T.astype(BF16)
@@ -290,15 +305,17 @@
 
     def power_of(channel, total):
         def add(group, total):
-            v = tiles[channel, pl.ds(pl.multiple_of(group * 16, 16), 16)].astype(F32)
+            v = tiles[channel, group // 4, pl.ds(pl.multiple_of((group % 4) * 16, 16), 16)].astype(F32)
             return total + jnp.sum(v * v, axis=0)
 
-        return lax.fori_loop(0, 8, add, total)
+        return lax.fori_loop(0, 8, add, total, unroll=True)
 
     def turn(channel):
         def pairs(pair, carry):
             sides = [
-                tiles[channel, pl.ds(pl.multiple_of(pair * 32 + side * 16, 16), 16)].reshape(256, LANES)
+                tiles[
+                    channel, pair // 2, pl.ds(pl.multiple_of(pair % 2 * 32 + side * 16, 16), 16)
+                ].reshape(256, LANES)
                 for side in range(2)
             ]
             moved = dot(swap[...], jnp.concatenate(sides, axis=1)).astype(BF16)
@@ -310,13 +327,13 @@
                     ]
             return carry
 
-        lax.fori_loop(0, 4, pairs, 0)
-
-    def turn_back(channel):
+        lax.fori_loop(0, 4, pairs, 0, unroll=True)
+
+    def turn_back(channel, which, put):
         def pairs(pair, carry):
             sides = []
             for side in range(2):
-                at = pl.ds(pl.multiple_of(pair * 32 + side * 16, 16), 16)
+                at = pl.ds(pl.multiple_of(which * CHIPS + pair * 32 + side * 16, 16), 16)
                 lines = [
                     turned[channel, r // 2, at, (r % 2) * LANES : (r % 2 + 1) * LANES]
                     for r in range(TILE)
@@ -325,10 +342,23 @@
             moved = dot(swap[...], jnp.concatenate(sides, axis=1)).astype(BF16)
             for side in range(2):
                 at = pl.ds(pl.multiple_of(pair * 32 + side * 16, 16), 16)
-                mixed[channel, at] = moved[:, side * LANES : (side + 1) * LANES].reshape(16, TILE, LANES)
+                put(at, moved[:, side * LANES : (side + 1) * LANES].reshape(16, TILE, LANES))
             return carry
 
-        lax.fori_loop(0, 4, pairs, 0)
+        lax.fori_loop(0, 2, pairs, 0, unroll=True)
+
+    def turn_back_other(channel):
+        def put(at, block):
+            mixed[channel, at] = block
+
+        turn_back(channel, 1 - core, put)
+        swap_mixed(channel).start()
+
+    def turn_back_own(channel):
+        def put(at, block):
+            joined[channel, at, :, core_lanes] = block
+
+        turn_back(channel, core, put)
 
     copy_here(tiles.at[0], tiles.at[0], go_recv.at[0]).wait()
     power = power_of(0, jnp.zeros((TILE, LANES), F32))
@@ -338,7 +368,7 @@
         inner[pair] = dot(w_in_t[:, :128], turned[0, pair])
         return carry
 
-    lax.fori_loop(0, TILE // 2, layer_part, 0)
+    lax.fori_loop(0, TILE // 2, layer_part, 0, unroll=True)
     copy_here(tiles.at[1], tiles.at[1], go_recv.at[1]).wait()
     power = power_of(1, power)
     scale[...] = lax.rsqrt(power * (1.0 / 256) + 1e-06)
@@ -353,16 +383,18 @@
         turned[1, pair] = result[128:]
         return carry
 
-    lax.fori_loop(0, TILE // 2, layers, 0)
+    lax.fori_loop(0, TILE // 2, layers, 0, unroll=True)
+    turn_back_other(0)
+    turn_back_other(1)
+    turn_back_own(0)
+    swap_mixed(0).wait_recv()
+    return_tiles(0)
+    turn_back_own(1)
+    swap_mixed(1).wait_recv()
+    return_tiles(1)
+
     for channel in range(2):
-        turn_back(channel)
-        return_tiles(channel)
-
-    for channel in range(2):
-        copy_here(returned.at[channel], returned.at[channel], ret_recv.at[channel]).wait()
-        final_copy(channel).start()
-        planes[channel, :, half_at(core)] = returned[channel, core]
-        final_copy(channel).wait_recv()
+        copy_here(planes.at[channel], planes.at[channel], ret_recv.at[channel]).wait()
         filter_plane(
             planes.at[channel], stepped.at[channel],
             lambda a, b: taps[a, b, (chip * 2 + core) * 2 + channel], out.at[channel], wide,
@@ -370,8 +402,8 @@
         copy_here(out.at[channel], out_h.at[channel], out_sem.at[channel]).start()
     for channel in range(2):
         pair_copy(channel).wait_send()
-        final_copy(channel).wait_send()
-        sent = tiles.at[channel, pl.ds(0, 2 * CHIPS - 2)]
+        swap_mixed(channel).wait_send()
+        sent = tiles.at[channel, :, pl.ds(0, CHIPS - 1)]
         copy_here(sent, sent, go_send.at[channel]).wait()
         copy_here(sent, sent, ret_send.at[channel]).wait()
         copy_here(out.at[channel], out_h.at[channel], out_sem.at[channel]).wait()
@@ -379,17 +411,23 @@
 
 def local(model, dirty, psf, step_size, gain, w_in, b_in, w_out, kernel):
     rows_in, cols_in, cols_out, rows_out, swap, order = make_tables()
-    smem = pl.BlockSpec(memory_space=pltpu.SMEM)
-    vmem = pl.BlockSpec(memory_space=pltpu.VMEM)
     hbm = pl.BlockSpec(memory_space=pl.ANY)
     dma = pltpu.SemaphoreType.DMA
     steps = LEN // STEP_COLS
     return pl.pallas_call(
         whole,
         out_shape=jax.ShapeDtypeStruct((2, IMG, IMG), BF16),
-        in_specs=[smem] * 2 + [hbm] * 7 + [vmem] * 6,
+        in_specs=[hbm] * 15,
         out_specs=hbm,
         scratch_shapes=[
+            pltpu.SMEM((2,), F32),
+            pltpu.SMEM((3, 3, 256), F32),
+            pltpu.VMEM((256, 256), BF16),
+            pltpu.VMEM((256, 256), BF16),
+            pltpu.VMEM((1, 256), F32),
+            pltpu.VMEM((256, 256), BF16),
+            pltpu.VMEM((1, 256), F32),
+            pltpu.VMEM((256, 256), BF16),
             pltpu.VMEM((2, IMG, IMG), BF16),
             pltpu.VMEM((2, IMG, IMG), BF16),
             pltpu.VMEM((2, PSF, PSF), BF16),
@@ -404,16 +442,16 @@
             pltpu.VMEM((2, IMG, IMG), BF16),
             pltpu.VMEM((2, 2, IMG, 256), BF16),
             pltpu.VMEM((2, IMG, 256), BF16),
-            pltpu.VMEM((2, 128, TILE, LANES), BF16),
+            pltpu.VMEM((2, 2, CHIPS, TILE, LANES), BF16),
             pltpu.VMEM((2, TILE // 2, 128, 256), BF16),
             pltpu.VMEM((TILE // 2, 256, 256), F32),
             pltpu.VMEM((TILE, LANES), F32),
-            pltpu.VMEM((2, 128, TILE, LANES), BF16),
-            pltpu.VMEM((2, 2, IMG, 256), BF16),
+            pltpu.VMEM((2, CHIPS, TILE, LANES), BF16),
+            pltpu.VMEM((2, CHIPS, TILE, 2 * LANES), BF16),
             pltpu.VMEM((2, IMG, IMG), BF16),
             pltpu.VMEM((2, IMG, IMG), BF16),
             pltpu.VMEM((IMG + 16, IMG), F32),
-            dma((8,)),
+            dma((16,)),
         ]
         + [dma((2,))] * 9,
         compiler_params=pltpu.CompilerParams(

time: 58.5 us -> 54.8 us (0.937)
  Pallas kernels: 56.1 us -> 52.4 us
    pallas_call x1, Pallas kernels: 56.1 us -> 52.4 us  [local(): pl.pallas_call(whole, out_shape=jax.ShapeDtypeStruct((2, IMG, IMG), BF16)...]
where the time goes in v3:
time: 54.8 us; the launch traced here: 54.6 us
  Pallas kernels  52.4 us (96%)
  local copies, waits for them, and re-layouts  2.26 us (4%)
    pallas_call x1, Pallas kernels, local(): pl.pallas_call(whole, out_shape=jax.ShapeDtypeStruct((2, IMG, IMG), BF16)...  52.4 us
    unnamed x1, local copies, waits for them, and re-layouts  2.26 us

profile of v3, /device:TPU:1, one launch (start us, length us, event | category | flops | bytes accessed | tf_op | source)
XLA Modules:
  0.0 54.6 jit_solution(448573408403262869)
XLA Ops:
  0.0 52.4 %shard_map.145 = bf16[2,512,512]{2,1,0:T(8,128)(2,1)} custom-call(f32[2]{0:T(128)} %rate_h.1, f32[3,3,256]{2,1,0:T(4,128)} %taps_h.1, bf16[2,512,512]{2,1,0:T(8,128)(2,1)} %model_h.1, bf16[2,512,512]{2,1,0:T(8,128)(2,1)} %dirty_h.1, bf16[2,256,256]{2,1,0:T(8,128)(2,1)} %psf_h.1, bf16[640,512]{1,0:T(8,128)(2,1)} %constant.12.clone.rows_in_h, ...), custom_call_target="tpu_custom_call" | custom-call | tf_op jit(solution)/shard_map/pallas_call | solution.py:417
  52.4 2.3 %copy.17 = bf16[2,512,512]{2,1,0:T(8,128)(2,1)} copy(bf16[2,512,512]{2,1,0:T(8,128)(2,1)} %shard_map.145) | data formatting | bytes 2097152

commit v4 on v3

v4 whole, which is shorter than its diff:
```python
import math

import jax
import jax.numpy as jnp
import ml_dtypes
import numpy as np
from jax import lax
from jax.experimental import pallas as pl
from jax.experimental.pallas import tpu as pltpu
from jax.sharding import PartitionSpec as P

BF16 = jnp.bfloat16
F32 = jnp.float32
MESH = pl.DeviceIdType.MESH
IMG = 512
PSF = 256
LEN = IMG + PSF // 2
HALF = LEN // 2
TILE = 16
LANES = 128
CHIPS = 64
FIVE = LEN // LANES


def angle(freq, place):
    turns = (2.0 * freq[:, None]) * place[None, :]
    return np.mod(turns, 2 * LEN) * (math.pi / LEN)


def make_tables():
    odd = np.arange(HALF) + 0.5
    even = np.arange(LEN).astype(np.float64)
    place = np.arange(IMG).astype(np.float64)
    window = place + PSF // 2
    first = angle(odd, place)
    rows_in = np.concatenate([np.cos(first), -np.sin(first)], axis=0)
    inside = np.arange(LANES).astype(np.float64)
    cols_in, cols_out = [], []
    for shift in range(FIVE):
        second = angle(even[shift::FIVE], inside)
        cos, sin = np.cos(second.T), np.sin(second.T)
        cols_in.append(np.block([[cos, -sin], [sin, cos]]))
        cos, sin = np.cos(second), np.sin(second)
        cols_out.append(np.block([[cos, sin], [-sin, cos]]))
    cols_in, cols_out = np.stack(cols_in), np.stack(cols_out)
    last = angle(odd, window).T
    rows_out = np.concatenate([2 * np.cos(last), -2 * np.sin(last)], axis=1)
    swap = np.zeros((256, 256))
    index = np.arange(256)
    swap[index, (index % 16) * 16 + index // 16] = 1
    order = np.zeros((256, 256))
    order[index, (index % 2) * 128 + (index // 2 % 2) * CHIPS + index // 4] = 1
    tables = (rows_in, cols_in, cols_out, rows_out, swap, order)
    return [x.astype(ml_dtypes.bfloat16) for x in tables]


def dot(a, b):
    return jnp.dot(a, b, preferred_element_type=F32)


def copy_here(src, dst, sem):
    return pltpu.make_async_copy(src, dst, sem)


COS = [math.cos(2 * math.pi * k / FIVE) for k in range(FIVE)]
SIN = [math.sin(2 * math.pi * k / FIVE) for k in range(FIVE)]


def combine(zero, ones, real_even, imag_odd):
    even = [zero[p] + ones[0] * real_even[0][p] + ones[1] * real_even[1][p] for p in range(2)]
    odd = [ones[2] * imag_odd[0][p] + ones[3] * imag_odd[1][p] for p in range(2)]
    plus = (even[0] - odd[1], even[1] + odd[0])
    minus = (even[0] + odd[1], even[1] - odd[0])
    return plus, minus


def spread_five(x):
    both = [x[2][p] + x[3][p] for p in range(2)]
    apart = [x[2][p] - x[3][p] for p in range(2)]
    fourth, first = combine(x[0], (COS[1], COS[2], SIN[1], SIN[2]), (x[1], both), (x[1], apart))
    third, second = combine(x[0], (COS[2], COS[1], SIN[2], -SIN[1]), (x[1], both), (x[1], apart))
    zeroth = tuple(x[0][p] + x[1][p] + both[p] for p in range(2))
    return zeroth, first, second, third, fourth


def spread_two(x):
    out = [tuple(x[0][p] + x[1][p] for p in range(2))]
    for r in range(1, FIVE):
        out.append(
            (
                x[0][0] + COS[r] * x[1][0] + SIN[r] * x[1][1],
                x[0][1] + COS[r] * x[1][1] - SIN[r] * x[1][0],
            )
        )
    return out


def gather_five(z):
    sums = [[z[k][p] + z[FIVE - k][p] for p in range(2)] for k in (1, 2)]
    gaps = [[z[k][p] - z[FIVE - k][p] for p in range(2)] for k in (1, 2)]
    first, fourth = combine(z[0], (COS[1], COS[2], SIN[1], SIN[2]), sums, gaps)
    second, third = combine(z[0], (COS[2], COS[1], SIN[2], -SIN[1]), sums, gaps)
    return first, second, third, fourth


def lane_blocks(ref, at_re, at_im, count):
    return [
        (ref[at_re, a * LANES : (a + 1) * LANES], ref[at_im, a * LANES : (a + 1) * LANES])
        for a in range(count)
    ]


def first_axis(plane, psf, rows_in, image, point, low, low_psf):
    low_psf[...] = dot(rows_in[:, :PSF], psf[...])
    low[...] = dot(rows_in[...], plane[...])

    def rows(step, carry):
        at = pl.multiple_of(step * 16, 16)
        at_re, at_im = pl.ds(at, 16), pl.ds(HALF + at, 16)
        for ref, out, spread in ((low_psf, point, spread_two), (low, image, spread_five)):
            parts = spread(lane_blocks(ref, at_re, at_im, ref.shape[1] // LANES))
            for r in range(FIVE):
                out[r, at_re, :LANES] = parts[r][0].astype(BF16)
                out[r, at_re, LANES:] = parts[r][1].astype(BF16)
        return carry

    lax.fori_loop(0, HALF // 16, rows, 0, unroll=4)


def second_axis(cols_in, cols_out, image, point, spectra):
    for r in range(FIVE):
        x = dot(image[r], cols_in[r]) * (1.0 / (LEN * LEN))
        q = dot(point[r], cols_in[r])
        real_x, imag_x = x[:, :LANES], x[:, LANES:]
        real_q, imag_q = q[:, :LANES], q[:, LANES:]
        real_p = (real_x * real_q - imag_x * imag_q).astype(BF16)
        imag_p = (real_x * imag_q + imag_x * real_q).astype(BF16)
        spectra[r] = dot(jnp.concatenate([real_p, imag_p], axis=1), cols_out[r])


def second_axis_back(spectra, back):
    def rows(step, carry):
        at = pl.multiple_of(step * 16, 16)
        here = pl.ds(at, 16)
        z = [(spectra[r, here, :LANES], spectra[r, here, LANES:]) for r in range(FIVE)]
        for a, (re, im) in enumerate(gather_five(z)):
            back[here, a * LANES : (a + 1) * LANES] = re.astype(BF16)
            back[pl.ds(HALF + at, 16), a * LANES : (a + 1) * LANES] = im.astype(BF16)
        return carry

    lax.fori_loop(0, HALF // 16, rows, 0, unroll=4)


def widen(units, half, wide):
    def some(step, carry):
        at = pl.multiple_of(step * 64, 64)
        v = units[pl.ds(at, 64), :].astype(F32).reshape(4, 2, 8, IMG)
        for channel in range(2):
            for g in range(4):
                wide[channel, pl.ds(at + g * 16 + half * 8 + 8, 8), :] = v[g, channel]
        return carry

    lax.fori_loop(0, IMG // 64, some, 0, unroll=4)


def filter_plane(stepped, taps, out, wide):
    rows = 32
    lane = lax.broadcasted_iota(jnp.int32, (rows, IMG), 1)

    def block(step, carry):
        at = pl.multiple_of(step * rows, rows)
        span = wide[pl.ds(at, rows + 16), :]
        lines = [span[7 + a : 7 + a + rows] for a in range(3)]
        sums = [sum(taps(a, b) * lines[a] for a in range(3)) for b in range(3)]
        left = jnp.where(lane == 0, 0.0, pltpu.roll(sums[0], 1, 1))
        right = jnp.where(lane == IMG - 1, 0.0, pltpu.roll(sums[2], IMG - 1, 1))
        total = stepped[pl.ds(at, rows), :].astype(F32) + (sums[1] + (left + right))
        out[pl.ds(at, rows), :] = total.astype(BF16)
        return carry

    lax.fori_loop(0, IMG // rows, block, 0, unroll=4)


def whole(
    rate_h, taps_h, model_h, dirty_h, psf_h, rows_in_h, cols_in_h, cols_out_h, rows_out_h,
    swap_h, order_h, gain_h, w_in_h, b_in_h, w_out_h, out_h,
    rate, taps, swap, order, gain, w_in, b_in, w_out,
    model, dirty, psf, rows_in, cols_in, cols_out, rows_out,
    low, low_psf, image, point, spectra, back, stepped, halves, parcel, tiles, turned,
    mixed, joined, planes, out, wide,
    load_sem, out_sem, pair_send, pair_recv, go_send, go_recv, ret_send, ret_recv, fin_send, fin_recv,
):
    row_at, col_at = lax.axis_index("rows"), lax.axis_index("cols")
    chip = row_at * 8 + col_at // 2
    core = col_at % 2
    sibling = {"rows": row_at, "cols": col_at + 1 - 2 * core}

    def at_chip(other):
        return {"rows": other // 8, "cols": (other % 8) * 2 + core}

    loads = []
    for src, dst in (
        (rows_in_h, rows_in),
        (model_h.at[0], model.at[0]),
        (psf_h, psf),
        (cols_in_h, cols_in),
        (cols_out_h, cols_out),
        (rows_out_h, rows_out),
        (dirty_h, dirty),
        (model_h.at[1], model.at[1]),
        (rate_h, rate),
        (swap_h, swap),
        (order_h, order),
        (gain_h, gain),
        (w_in_h, w_in),
        (b_in_h, b_in),
        (w_out_h, w_out),
        (taps_h, taps),
    ):
        copy = copy_here(src, dst, load_sem.at[len(loads)])
        copy.start()
        loads.append(copy)

    barrier = pltpu.get_barrier_semaphore()
    pl.semaphore_signal(barrier, inc=1, device_id=sibling, device_id_type=MESH)

    def greet(k, carry):
        pl.semaphore_signal(barrier, inc=1, device_id=at_chip(chip ^ k), device_id_type=MESH)
        return carry

    lax.fori_loop(1, CHIPS, greet, 0)

    def pair_copy(half, at):
        return pltpu.make_async_remote_copy(
            src_ref=parcel.at[half, at],
            dst_ref=halves.at[half, core, at],
            send_sem=pair_send.at[half],
            recv_sem=pair_recv.at[half],
            device_id=sibling,
            device_id_type=MESH,
        )

    def ahead(channel, at):
        blurred = dot(rows_out[at, :], back[...])
        held = model[channel, at, :].astype(F32)
        result = held + rate[channel] * (dirty[channel, at, :].astype(F32) - blurred)
        result = result.astype(BF16)
        stepped[channel, at, :] = result
        return result

    def pack(at):
        planes_at = [stepped[0, at, :].astype(F32), ahead(1, at).astype(F32)]
        planes_at = [v.reshape(8, 2, 8, IMG) for v in planes_at]
        for half in range(2):
            unit = jnp.stack([v[:, half] for v in planes_at], axis=1).reshape(128, IMG).astype(BF16)
            first = jnp.concatenate([unit[:, :128], unit[:, 256:384]], axis=1)
            second = jnp.concatenate([unit[:, 128:256], unit[:, 384:]], axis=1)
            halves[half, core, at, :] = jnp.where(core == 0, first, second)
            parcel[half, at, :] = jnp.where(core == 0, second, first)
        for half in range(2):
            pair_copy(half, at).start()

    def tile_of(planes_ref, other):
        at = pl.ds(pl.multiple_of((other // 2) * TILE, TILE), TILE)
        return planes_ref.at[:, at, pl.ds(pl.multiple_of((other % 2) * LANES, LANES), LANES)]

    def place_of(plane_ref, other):
        at = pl.ds(pl.multiple_of((other // 2) * TILE, TILE), TILE)
        return plane_ref.at[at, pl.ds(pl.multiple_of((other % 2) * 256, 256), 256)]

    core_lanes = pl.ds(pl.multiple_of(core * LANES, LANES), LANES)

    def send_tiles(channel):
        def send(k, carry):
            other = chip ^ k
            pltpu.make_async_remote_copy(
                src_ref=tile_of(halves.at[channel], other),
                dst_ref=tiles.at[channel, :, chip],
                send_sem=go_send.at[channel],
                recv_sem=go_recv.at[channel],
                device_id=at_chip(other),
                device_id_type=MESH,
            ).start()
            return carry

        lax.fori_loop(1, CHIPS, send, 0)
        copy_here(
            tile_of(halves.at[channel], chip),
            tiles.at[channel, :, chip],
            go_recv.at[channel],
        ).start()

    def return_tiles(channel):
        def send(k, carry):
            other = chip ^ k
            pltpu.make_async_remote_copy(
                src_ref=joined.at[channel, other],
                dst_ref=place_of(planes.at[channel], chip),
                send_sem=ret_send.at[channel],
                recv_sem=ret_recv.at[channel],
                device_id=at_chip(other),
                device_id_type=MESH,
            ).start()
            return carry

        lax.fori_loop(1, CHIPS, send, 0)
        copy_here(
            joined.at[channel, chip],
            place_of(planes.at[channel], chip),
            ret_recv.at[channel],
        ).start()

    def swap_mixed(channel):
        return pltpu.make_async_remote_copy(
            src_ref=mixed.at[channel],
            dst_ref=joined.at[channel, :, :, core_lanes],
            send_sem=fin_send.at[channel],
            recv_sem=fin_recv.at[channel],
            device_id=sibling,
            device_id_type=MESH,
        )

    for load in loads[:3]:
        load.wait()
    first_axis(model.at[0], psf.at[0], rows_in, image, point, low, low_psf)
    loads[3].wait()
    loads[4].wait()
    second_axis(cols_in, cols_out, image, point, spectra)
    second_axis_back(spectra, back)
    loads[5].wait()
    loads[6].wait()
    loads[8].wait()
    blocks = [pl.ds(step * 128, 128) for step in range(IMG // 128)]
    for at in blocks:
        ahead(0, at)
    loads[7].wait()
    first_axis(model.at[1], psf.at[1], rows_in, image, point, low, low_psf)
    second_axis(cols_in, cols_out, image, point, spectra)
    second_axis_back(spectra, back)
    pl.semaphore_wait(barrier, CHIPS)
    for at in blocks:
        pack(at)
    for half in range(2):
        copy_here(parcel.at[half], parcel.at[half], pair_recv.at[half]).wait()
        send_tiles(half)

    for load in loads[9:]:
        load.wait()
    w_in_t = (w_in[...].astype(F32).T * gain[...]).astype(BF16)
    w_in_t = dot(w_in_t, order[...]).astype(BF16)
    w_out_t = dot(w_out[...], order[...]).T.astype(BF16)
    bias = jnp.broadcast_to(b_in[...], (LANES, 256)).T
    bias = jnp.concatenate([bias, bias], axis=1)

    def scale_of(half):
        total = jnp.zeros((TILE, LANES), F32)
        for group in range(8):
            v = tiles[half, group // 4, pl.ds(group % 4 * 16, 16)].astype(F32)
            total = total + jnp.sum(v * v, axis=0)
        return lax.rsqrt((total[:8] + total[8:]) * (1.0 / 256) + 1e-06)

    def turn(half):
        for pair in range(4):
            sides = [
                tiles[half, pair // 2, pl.ds(pair % 2 * 32 + side * 16, 16)].reshape(256, LANES)
                for side in range(2)
            ]
            moved = dot(swap[...], jnp.concatenate(sides, axis=1)).astype(BF16)
            for side in range(2):
                for line in range(TILE):
                    channel, r = divmod(line, 8)
                    at = pl.ds(channel * 128 + pair * 32 + side * 16, 16)
                    turned[half, r // 2, at, (r % 2) * LANES : (r % 2 + 1) * LANES] = moved[
                        line * 16 : (line + 1) * 16, side * LANES : (side + 1) * LANES
                    ]

    def layers(half):
        scale = scale_of(half)
        for pair in range(4):
            factor = jnp.concatenate(
                [scale[2 * pair : 2 * pair + 1], scale[2 * pair + 1 : 2 * pair + 2]], axis=1
            )
            total = dot(w_in_t, turned[half, pair])
            hidden = jax.nn.gelu(total * factor + bias, approximate=True).astype(BF16)
            turned[half, pair] = dot(w_out_t, hidden).astype(BF16)

    def turn_back(half, which, put):
        for pair in range(2):
            sides = []
            for side in range(2):
                lines = []
                for line in range(TILE):
                    channel, r = divmod(line, 8)
                    first = channel * 128 + pair * 32 + side * 16
                    at = pl.ds(pl.multiple_of(which * CHIPS + first, 16), 16)
                    lines.append(turned[half, r // 2, at, (r % 2) * LANES : (r % 2 + 1) * LANES])
                sides.append(jnp.concatenate(lines, axis=0))
            moved = dot(swap[...], jnp.concatenate(sides, axis=1)).astype(BF16)
            for side in range(2):
                block = moved[:, side * LANES : (side + 1) * LANES].reshape(16, TILE, LANES)
                put(pl.ds(pair * 32 + side * 16, 16), block)

    def turn_back_other(half):
        def put(at, block):
            mixed[half, at] = block

        turn_back(half, 1 - core, put)
        swap_mixed(half).start()

    def turn_back_own(half):
        def put(at, block):
            joined[half, at, :, core_lanes] = block

        turn_back(half, core, put)

    for half in range(2):
        copy_here(tiles.at[half], tiles.at[half], go_recv.at[half]).wait()
        turn(half)
        layers(half)
        turn_back_other(half)
        turn_back_own(half)
        swap_mixed(half).wait_recv()
        return_tiles(half)

    zero = jnp.zeros((8, IMG), F32)
    for channel in range(2):
        wide[channel, :8] = zero
        wide[channel, 8 + IMG :] = zero
    for half in range(2):
        copy_here(planes.at[half], planes.at[half], ret_recv.at[half]).wait()
        widen(planes.at[half], half, wide)
    for channel in range(2):
        filter_plane(
            stepped.at[channel],
            lambda a, b: taps[a, b, (chip * 2 + core) * 2 + channel], out.at[channel], wide.at[channel],
        )
        copy_here(out.at[channel], out_h.at[channel], out_sem.at[channel]).start()
    for channel in range(2):
        copy_here(parcel.at[channel], parcel.at[channel], pair_send.at[channel]).wait()
        swap_mixed(channel).wait_send()
        sent = tiles.at[channel, :, pl.ds(0, CHIPS - 1)]
        copy_here(sent, sent, go_send.at[channel]).wait()
        copy_here(sent, sent, ret_send.at[channel]).wait()
        copy_here(out.at[channel], out_h.at[channel], out_sem.at[channel]).wait()


def local(model, dirty, psf, step_size, gain, w_in, b_in, w_out, kernel):
    rows_in, cols_in, cols_out, rows_out, swap, order = make_tables()
    hbm = pl.BlockSpec(memory_space=pl.ANY)
    dma = pltpu.SemaphoreType.DMA
    return pl.pallas_call(
        whole,
        out_shape=jax.ShapeDtypeStruct((2, IMG, IMG), BF16),
        in_specs=[hbm] * 15,
        out_specs=hbm,
        scratch_shapes=[
            pltpu.SMEM((2,), F32),
            pltpu.SMEM((3, 3, 256), F32),
            pltpu.VMEM((256, 256), BF16),
            pltpu.VMEM((256, 256), BF16),
            pltpu.VMEM((1, 256), F32),
            pltpu.VMEM((256, 256), BF16),
            pltpu.VMEM((1, 256), F32),
            pltpu.VMEM((256, 256), BF16),
            pltpu.VMEM((2, IMG, IMG), BF16),
            pltpu.VMEM((2, IMG, IMG), BF16),
            pltpu.VMEM((2, PSF, PSF), BF16),
            pltpu.VMEM(rows_in.shape, BF16),
            pltpu.VMEM(cols_in.shape, BF16),
            pltpu.VMEM(cols_out.shape, BF16),
            pltpu.VMEM(rows_out.shape, BF16),
            pltpu.VMEM((LEN, IMG), F32),
            pltpu.VMEM((LEN, PSF), F32),
            pltpu.VMEM((FIVE, HALF, 2 * LANES), BF16),
            pltpu.VMEM((FIVE, HALF, 2 * LANES), BF16),
            pltpu.VMEM((FIVE, HALF, 2 * LANES), F32),
            pltpu.VMEM((LEN, IMG), BF16),
            pltpu.VMEM((2, IMG, IMG), BF16),
            pltpu.VMEM((2, 2, IMG, 256), BF16),
            pltpu.VMEM((2, IMG, 256), BF16),
            pltpu.VMEM((2, 2, CHIPS, TILE, LANES), BF16),
            pltpu.VMEM((2, TILE // 4, 256, 256), BF16),
            pltpu.VMEM((2, CHIPS, TILE, LANES), BF16),
            pltpu.VMEM((2, CHIPS, TILE, 2 * LANES), BF16),
            pltpu.VMEM((2, IMG, IMG), BF16),
            pltpu.VMEM((2, IMG, IMG), BF16),
            pltpu.VMEM((2, IMG + 16, IMG), F32),
            dma((16,)),
        ]
        + [dma((2,))] * 9,
        compiler_params=pltpu.CompilerParams(
            vmem_limit_bytes=64 << 20, collective_id=0, has_side_effects=True
        ),
    )(
        step_size, kernel, model, dirty, psf, rows_in, cols_in, cols_out, rows_out,
        swap, order, gain[None, :], w_in, b_in[None, :], w_out,
    )


def solution(mesh):
    split = P(("rows", "cols"), None, None)
    return jax.shard_map(
        local,
        mesh=mesh,
        in_specs=(split, split, split, P(("rows", "cols")), P(), P(), P(), P(), P()),
        out_specs=split,
        check_vma=False,
    )
```

time: 54.8 us -> 50.5 us (0.922)
  Pallas kernels: 52.4 us -> 48.1 us
    pallas_call x1, Pallas kernels: 52.4 us -> 48.1 us  [local(): pl.pallas_call(whole, out_shape=jax.ShapeDtypeStruct((2, IMG, IMG), BF16)...]
where the time goes in v4:
time: 50.5 us; the launch traced here: 50.3 us
  Pallas kernels  48.1 us (95%)
  local copies, waits for them, and re-layouts  2.26 us (4%)
    pallas_call x1, Pallas kernels, local(): pl.pallas_call(whole, out_shape=jax.ShapeDtypeStruct((2, IMG, IMG), BF16)...  48.1 us
    unnamed x1, local copies, waits for them, and re-layouts  2.26 us

profile of v4, /device:TPU:1, one launch (start us, length us, event | category | flops | bytes accessed | tf_op | source)
XLA Modules:
  0.0 50.3 jit_solution(6718153177884910298)
XLA Ops:
  0.0 48.1 %shard_map.145 = bf16[2,512,512]{2,1,0:T(8,128)(2,1)} custom-call(f32[2]{0:T(128)} %rate_h.1, f32[3,3,256]{2,1,0:T(4,128)} %taps_h.1, bf16[2,512,512]{2,1,0:T(8,128)(2,1)} %model_h.1, bf16[2,512,512]{2,1,0:T(8,128)(2,1)} %dirty_h.1, bf16[2,256,256]{2,1,0:T(8,128)(2,1)} %psf_h.1, bf16[640,512]{1,0:T(8,128)(2,1)} %constant.12.clone.rows_in_h, ...), custom_call_target="tpu_custom_call" | custom-call | tf_op jit(solution)/shard_map/pallas_call | solution.py:451
  48.1 2.3 %copy.17 = bf16[2,512,512]{2,1,0:T(8,128)(2,1)} copy(bf16[2,512,512]{2,1,0:T(8,128)(2,1)} %shard_map.145) | data formatting | bytes 2097152

commit v5 on v4

--- a/solution.py
+++ b/solution.py
@@ -16,6 +16,8 @@
 PSF = 256
 LEN = IMG + PSF // 2
 HALF = LEN // 2
+PARTS = 4
+BLOCKS = 4
 TILE = 16
 LANES = 128
 CHIPS = 64
@@ -124,7 +126,7 @@
                 out[r, at_re, LANES:] = parts[r][1].astype(BF16)
         return carry
 
-    lax.fori_loop(0, HALF // 16, rows, 0, unroll=4)
+    lax.fori_loop(0, HALF // 16, rows, 0, unroll=True)
 
 
 def second_axis(cols_in, cols_out, image, point, spectra):
@@ -148,37 +150,49 @@
             back[pl.ds(HALF + at, 16), a * LANES : (a + 1) * LANES] = im.astype(BF16)
         return carry
 
-    lax.fori_loop(0, HALF // 16, rows, 0, unroll=4)
-
-
-def widen(units, half, wide):
+    lax.fori_loop(0, HALF // 16, rows, 0, unroll=True)
+
+
+def filter_columns(units, half, taps, wide):
+    lane = lax.broadcasted_iota(jnp.int32, (8, LANES), 1)
+    zero = jnp.zeros((8, LANES), F32)
+    weights = [[[taps(a, b, channel) for b in range(3)] for a in range(3)] for channel in range(2)]
+
     def some(step, carry):
         at = pl.multiple_of(step * 64, 64)
         v = units[pl.ds(at, 64), :].astype(F32).reshape(4, 2, 8, IMG)
         for channel in range(2):
+            w = weights[channel]
             for g in range(4):
-                wide[channel, pl.ds(at + g * 16 + half * 8 + 8, 8), :] = v[g, channel]
+                to = pl.ds(at + g * 16 + half * 8 + 8, 8)
+                m = [v[g, channel, :, j * LANES : (j + 1) * LANES] for j in range(BLOCKS)]
+                left = [zero] + [pltpu.roll(x, 1, 1) for x in m]
+                right = [pltpu.roll(x, LANES - 1, 1) for x in m] + [zero]
+                for j in range(BLOCKS):
+                    before = jnp.where(lane == 0, left[j], left[j + 1])
+                    after = jnp.where(lane == LANES - 1, right[j + 1], right[j])
+                    for a in range(3):
+                        wide[a, channel, j, to, :] = (
+                            w[a][0] * before + w[a][1] * m[j] + w[a][2] * after
+                        )
         return carry
 
-    lax.fori_loop(0, IMG // 64, some, 0, unroll=4)
-
-
-def filter_plane(stepped, taps, out, wide):
-    rows = 32
-    lane = lax.broadcasted_iota(jnp.int32, (rows, IMG), 1)
+    lax.fori_loop(0, IMG // 64, some, 0, unroll=2)
+
+
+def filter_rows(stepped, channel, out, wide, start, count):
+    rows = 16
 
     def block(step, carry):
-        at = pl.multiple_of(step * rows, rows)
-        span = wide[pl.ds(at, rows + 16), :]
-        lines = [span[7 + a : 7 + a + rows] for a in range(3)]
-        sums = [sum(taps(a, b) * lines[a] for a in range(3)) for b in range(3)]
-        left = jnp.where(lane == 0, 0.0, pltpu.roll(sums[0], 1, 1))
-        right = jnp.where(lane == IMG - 1, 0.0, pltpu.roll(sums[2], IMG - 1, 1))
-        total = stepped[pl.ds(at, rows), :].astype(F32) + (sums[1] + (left + right))
-        out[pl.ds(at, rows), :] = total.astype(BF16)
+        at = pl.multiple_of(start + step * rows, rows)
+        for j in range(BLOCKS):
+            lines = [wide[a, channel, j, pl.ds(at + 7 + a, rows), :] for a in range(3)]
+            lanes = slice(j * LANES, (j + 1) * LANES)
+            total = stepped[pl.ds(at, rows), lanes].astype(F32) + (lines[0] + lines[1] + lines[2])
+            out[pl.ds(at, rows), lanes] = total.astype(BF16)
         return carry
 
-    lax.fori_loop(0, IMG // rows, block, 0, unroll=4)
+    lax.fori_loop(0, count // rows, block, 0, unroll=True)
 
 
 def whole(
@@ -422,26 +436,32 @@
         swap_mixed(half).wait_recv()
         return_tiles(half)
 
-    zero = jnp.zeros((8, IMG), F32)
-    for channel in range(2):
-        wide[channel, :8] = zero
-        wide[channel, 8 + IMG :] = zero
+    zero = jnp.zeros((3, 2, BLOCKS, 8, LANES), F32)
+    wide[:, :, :, :8] = zero
+    wide[:, :, :, 8 + IMG :] = zero
+
+    def own_taps(a, b, channel):
+        return taps[a, b, (chip * 2 + core) * 2 + channel]
+
     for half in range(2):
         copy_here(planes.at[half], planes.at[half], ret_recv.at[half]).wait()
-        widen(planes.at[half], half, wide)
+        filter_columns(planes.at[half], half, own_taps, wide)
     for channel in range(2):
-        filter_plane(
-            stepped.at[channel],
-            lambda a, b: taps[a, b, (chip * 2 + core) * 2 + channel], out.at[channel], wide.at[channel],
-        )
-        copy_here(out.at[channel], out_h.at[channel], out_sem.at[channel]).start()
+        for part in range(PARTS):
+            rows = pl.ds(part * (IMG // PARTS), IMG // PARTS)
+            filter_rows(
+                stepped.at[channel], channel, out.at[channel], wide, part * (IMG // PARTS), IMG // PARTS
+            )
+            copy_here(out.at[channel, rows], out_h.at[channel, rows], out_sem.at[channel, part]).start()
     for channel in range(2):
         copy_here(parcel.at[channel], parcel.at[channel], pair_send.at[channel]).wait()
         swap_mixed(channel).wait_send()
         sent = tiles.at[channel, :, pl.ds(0, CHIPS - 1)]
         copy_here(sent, sent, go_send.at[channel]).wait()
         copy_here(sent, sent, ret_send.at[channel]).wait()
-        copy_here(out.at[channel], out_h.at[channel], out_sem.at[channel]).wait()
+        for part in range(PARTS):
+            rows = pl.ds(part * (IMG // PARTS), IMG // PARTS)
+            copy_here(out.at[channel, rows], out_h.at[channel, rows], out_sem.at[channel, part]).wait()
 
 
 def local(model, dirty, psf, step_size, gain, w_in, b_in, w_out, kernel):
@@ -484,10 +504,10 @@
             pltpu.VMEM((2, CHIPS, TILE, 2 * LANES), BF16),
             pltpu.VMEM((2, IMG, IMG), BF16),
             pltpu.VMEM((2, IMG, IMG), BF16),
-            pltpu.VMEM((2, IMG + 16, IMG), F32),
+            pltpu.VMEM((3, 2, BLOCKS, IMG + 16, LANES), F32),
             dma((16,)),
         ]
-        + [dma((2,))] * 9,
+        + [dma((2, PARTS))] + [dma((2,))] * 8,
         compiler_params=pltpu.CompilerParams(
             vmem_limit_bytes=64 << 20, collective_id=0, has_side_effects=True
         ),

time: 50.5 us -> 47.5 us (0.941)
  Pallas kernels: 48.1 us -> 45.1 us
    pallas_call x1, Pallas kernels: 48.1 us -> 45.1 us  [local(): pl.pallas_call(whole, out_shape=jax.ShapeDtypeStruct((2, IMG, IMG), BF16)...]
where the time goes in v5:
time: 47.5 us; the launch traced here: 47.4 us
  Pallas kernels  45.1 us (95%)
  local copies, waits for them, and re-layouts  2.26 us (5%)
    pallas_call x1, Pallas kernels, local(): pl.pallas_call(whole, out_shape=jax.ShapeDtypeStruct((2, IMG, IMG), BF16)...  45.1 us
    unnamed x1, local copies, waits for them, and re-layouts  2.26 us

profile of v5, /device:TPU:1, one launch (start us, length us, event | category | flops | bytes accessed | tf_op | source)
XLA Modules:
  0.0 47.4 jit_solution(18162323640555822494)
XLA Ops:
  0.0 45.1 %shard_map.145 = bf16[2,512,512]{2,1,0:T(8,128)(2,1)} custom-call(f32[2]{0:T(128)} %rate_h.1, f32[3,3,256]{2,1,0:T(4,128)} %taps_h.1, bf16[2,512,512]{2,1,0:T(8,128)(2,1)} %model_h.1, bf16[2,512,512]{2,1,0:T(8,128)(2,1)} %dirty_h.1, bf16[2,256,256]{2,1,0:T(8,128)(2,1)} %psf_h.1, bf16[640,512]{1,0:T(8,128)(2,1)} %constant.12.clone.rows_in_h, ...), custom_call_target="tpu_custom_call" | custom-call | tf_op jit(solution)/shard_map/pallas_call | solution.py:471
  45.1 2.3 %copy.17 = bf16[2,512,512]{2,1,0:T(8,128)(2,1)} copy(bf16[2,512,512]{2,1,0:T(8,128)(2,1)} %shard_map.145) | data formatting | bytes 2097152

commit v6 on v5

--- a/solution.py
+++ b/solution.py
@@ -214,14 +214,14 @@
 
     loads = []
     for src, dst in (
+        (psf_h, psf),
         (rows_in_h, rows_in),
         (model_h.at[0], model.at[0]),
-        (psf_h, psf),
+        (model_h.at[1], model.at[1]),
         (cols_in_h, cols_in),
         (cols_out_h, cols_out),
         (rows_out_h, rows_out),
         (dirty_h, dirty),
-        (model_h.at[1], model.at[1]),
         (rate_h, rate),
         (swap_h, swap),
         (order_h, order),
@@ -255,7 +255,7 @@
         )
 
     def ahead(channel, at):
-        blurred = dot(rows_out[at, :], back[...])
+        blurred = dot(rows_out[at, :], back[channel])
         held = model[channel, at, :].astype(F32)
         result = held + rate[channel] * (dirty[channel, at, :].astype(F32) - blurred)
         result = result.astype(BF16)
@@ -286,7 +286,7 @@
 
     def send_tiles(channel):
         def send(k, carry):
-            other = chip ^ k
+            other = chip ^ (CHIPS - k)
             pltpu.make_async_remote_copy(
                 src_ref=tile_of(halves.at[channel], other),
                 dst_ref=tiles.at[channel, :, chip],
@@ -306,7 +306,7 @@
 
     def return_tiles(channel):
         def send(k, carry):
-            other = chip ^ k
+            other = chip ^ (CHIPS - k)
             pltpu.make_async_remote_copy(
                 src_ref=joined.at[channel, other],
                 dst_ref=place_of(planes.at[channel], chip),
@@ -334,23 +334,30 @@
             device_id_type=MESH,
         )
 
-    for load in loads[:3]:
+    def first(channel):
+        first_axis(
+            model.at[channel], psf.at[channel], rows_in, image.at[channel], point.at[channel],
+            low.at[channel], low_psf.at[channel],
+        )
+
+    def second(channel):
+        second_axis(cols_in, cols_out, image.at[channel], point.at[channel], spectra.at[channel])
+
+    blocks = [pl.ds(step * 128, 128) for step in range(IMG // 128)]
+    for load in loads[:4]:
         load.wait()
-    first_axis(model.at[0], psf.at[0], rows_in, image, point, low, low_psf)
-    loads[3].wait()
-    loads[4].wait()
-    second_axis(cols_in, cols_out, image, point, spectra)
-    second_axis_back(spectra, back)
-    loads[5].wait()
-    loads[6].wait()
-    loads[8].wait()
-    blocks = [pl.ds(step * 128, 128) for step in range(IMG // 128)]
+    first(0)
+    first(1)
+    for load in loads[4:6]:
+        load.wait()
+    second(0)
+    second(1)
+    second_axis_back(spectra.at[0], back.at[0])
+    for load in loads[6:9]:
+        load.wait()
     for at in blocks:
         ahead(0, at)
-    loads[7].wait()
-    first_axis(model.at[1], psf.at[1], rows_in, image, point, low, low_psf)
-    second_axis(cols_in, cols_out, image, point, spectra)
-    second_axis_back(spectra, back)
+    second_axis_back(spectra.at[1], back.at[1])
     pl.semaphore_wait(barrier, CHIPS)
     for at in blocks:
         pack(at)
@@ -489,12 +496,12 @@
             pltpu.VMEM(cols_in.shape, BF16),
             pltpu.VMEM(cols_out.shape, BF16),
             pltpu.VMEM(rows_out.shape, BF16),
-            pltpu.VMEM((LEN, IMG), F32),
-            pltpu.VMEM((LEN, PSF), F32),
-            pltpu.VMEM((FIVE, HALF, 2 * LANES), BF16),
-            pltpu.VMEM((FIVE, HALF, 2 * LANES), BF16),
-            pltpu.VMEM((FIVE, HALF, 2 * LANES), F32),
-            pltpu.VMEM((LEN, IMG), BF16),
+            pltpu.VMEM((2, LEN, IMG), F32),
+            pltpu.VMEM((2, LEN, PSF), F32),
+            pltpu.VMEM((2, FIVE, HALF, 2 * LANES), BF16),
+            pltpu.VMEM((2, FIVE, HALF, 2 * LANES), BF16),
+            pltpu.VMEM((2, FIVE, HALF, 2 * LANES), F32),
+            pltpu.VMEM((2, LEN, IMG), BF16),
             pltpu.VMEM((2, IMG, IMG), BF16),
             pltpu.VMEM((2, 2, IMG, 256), BF16),
             pltpu.VMEM((2, IMG, 256), BF16),

time: 47.5 us -> 46 us (0.968)
  Pallas kernels: 45.1 us -> 43.6 us
    pallas_call x1, Pallas kernels: 45.1 us -> 43.6 us  [local(): pl.pallas_call(whole, out_shape=jax.ShapeDtypeStruct((2, IMG, IMG), BF16)...]
where the time goes in v6:
time: 46 us; the launch traced here: 45.9 us
  Pallas kernels  43.6 us (95%)
  local copies, waits for them, and re-layouts  2.26 us (5%)
    pallas_call x1, Pallas kernels, local(): pl.pallas_call(whole, out_shape=jax.ShapeDtypeStruct((2, IMG, IMG), BF16)...  43.6 us
    unnamed x1, local copies, waits for them, and re-layouts  2.26 us

profile of v6, /device:TPU:1, one launch (start us, length us, event | category | flops | bytes accessed | tf_op | source)
XLA Modules:
  0.0 45.9 jit_solution(1684574086232546685)
XLA Ops:
  0.0 43.6 %shard_map.145 = bf16[2,512,512]{2,1,0:T(8,128)(2,1)} custom-call(f32[2]{0:T(128)} %rate_h.1, f32[3,3,256]{2,1,0:T(4,128)} %taps_h.1, bf16[2,512,512]{2,1,0:T(8,128)(2,1)} %model_h.1, bf16[2,512,512]{2,1,0:T(8,128)(2,1)} %dirty_h.1, bf16[2,256,256]{2,1,0:T(8,128)(2,1)} %psf_h.1, bf16[640,512]{1,0:T(8,128)(2,1)} %constant.12.clone.rows_in_h, ...), custom_call_target="tpu_custom_call" | custom-call | tf_op jit(solution)/shard_map/pallas_call | solution.py:478
  43.6 2.3 %copy.17 = bf16[2,512,512]{2,1,0:T(8,128)(2,1)} copy(bf16[2,512,512]{2,1,0:T(8,128)(2,1)} %shard_map.145) | data formatting | bytes 2097152

commit v7 on v6

--- a/solution.py
+++ b/solution.py
@@ -262,17 +262,14 @@
         stepped[channel, at, :] = result
         return result
 
-    def pack(at):
-        planes_at = [stepped[0, at, :].astype(F32), ahead(1, at).astype(F32)]
-        planes_at = [v.reshape(8, 2, 8, IMG) for v in planes_at]
-        for half in range(2):
-            unit = jnp.stack([v[:, half] for v in planes_at], axis=1).reshape(128, IMG).astype(BF16)
-            first = jnp.concatenate([unit[:, :128], unit[:, 256:384]], axis=1)
-            second = jnp.concatenate([unit[:, 128:256], unit[:, 384:]], axis=1)
-            halves[half, core, at, :] = jnp.where(core == 0, first, second)
-            parcel[half, at, :] = jnp.where(core == 0, second, first)
-        for half in range(2):
-            pair_copy(half, at).start()
+    def pack(half, at):
+        v = [stepped[c, at, :].astype(F32).reshape(8, 2, 8, IMG)[:, half] for c in range(2)]
+        unit = jnp.stack(v, axis=1).reshape(128, IMG).astype(BF16)
+        first = jnp.concatenate([unit[:, :128], unit[:, 256:384]], axis=1)
+        second = jnp.concatenate([unit[:, 128:256], unit[:, 384:]], axis=1)
+        halves[half, core, at, :] = jnp.where(core == 0, first, second)
+        parcel[half, at, :] = jnp.where(core == 0, second, first)
+        pair_copy(half, at).start()
 
     def tile_of(planes_ref, other):
         at = pl.ds(pl.multiple_of((other // 2) * TILE, TILE), TILE)
@@ -360,7 +357,10 @@
     second_axis_back(spectra.at[1], back.at[1])
     pl.semaphore_wait(barrier, CHIPS)
     for at in blocks:
-        pack(at)
+        ahead(1, at)
+        pack(0, at)
+    for at in blocks:
+        pack(1, at)
     for half in range(2):
         copy_here(parcel.at[half], parcel.at[half], pair_recv.at[half]).wait()
         send_tiles(half)

time: 46 us -> 46 us (level)
  no operation moved by 1% of the time
where the time goes in v7:
time: 46 us; the launch traced here: 45.8 us
  Pallas kernels  43.5 us (95%)
  local copies, waits for them, and re-layouts  2.26 us (5%)
    pallas_call x1, Pallas kernels, local(): pl.pallas_call(whole, out_shape=jax.ShapeDtypeStruct((2, IMG, IMG), BF16)...  43.5 us
    unnamed x1, local copies, waits for them, and re-layouts  2.26 us

profile of v7, /device:TPU:1, one launch (start us, length us, event | category | flops | bytes accessed | tf_op | source)
XLA Modules:
  0.0 45.8 jit_solution(10389164075807185961)
XLA Ops:
  0.0 43.5 %shard_map.145 = bf16[2,512,512]{2,1,0:T(8,128)(2,1)} custom-call(f32[2]{0:T(128)} %rate_h.1, f32[3,3,256]{2,1,0:T(4,128)} %taps_h.1, bf16[2,512,512]{2,1,0:T(8,128)(2,1)} %model_h.1, bf16[2,512,512]{2,1,0:T(8,128)(2,1)} %dirty_h.1, bf16[2,256,256]{2,1,0:T(8,128)(2,1)} %psf_h.1, bf16[640,512]{1,0:T(8,128)(2,1)} %constant.12.clone.rows_in_h, ...), custom_call_target="tpu_custom_call" | custom-call | tf_op jit(solution)/shard_map/pallas_call | solution.py:478
  43.6 2.3 %copy.17 = bf16[2,512,512]{2,1,0:T(8,128)(2,1)} copy(bf16[2,512,512]{2,1,0:T(8,128)(2,1)} %shard_map.145) | data formatting | bytes 2097152
